TPU v7x, 32 devices: a whole 2x2x4 slice. The times are simulated.
32 devices in a mesh: seq: 8 (over y, x, core), tp: 4 (over z).
Axes of the slice: x: 2, y: 2, z: 4, core: 2. Of those that a mesh axis runs over, the one named last changes fastest.
Arguments:
- tokens: bfloat16 [1024, 8192], P('seq', 'tp'), may hold values from -6 to 6
- w_gate: bfloat16 [8192, 8192], P(None, 'tp'), may hold values from -0.09375 to 0.09375
- w_conv_in: bfloat16 [8192, 8192], P(None, 'tp'), may hold values from -0.09375 to 0.09375
- conv_weight: float32 [4, 8192], P(None, 'tp'), may hold values from -3 to 3
- conv_bias: float32 [8192], P('tp'), may hold values from -3 to 3
- score_head: bfloat16 [10, 8192], P(None, 'tp'), may hold values from -6 to 6
- targets: int32 [1024], P('seq'), may hold values from 0 to 9
- loss_mask: int32 [1024], P('seq'), may hold values 0 or 1
Outputs:
- gated: bfloat16 [1024, 8192], P('seq', 'tp')
- d_tokens: bfloat16 [1024, 8192], P('seq', 'tp')
All inputs are finite; a program needn't handle non-finite values. No bound on the sum of `loss_mask` on one device may be relied on, other than what follows from the above.
Results may differ from a plain program's by a relative error of at most 0.03.
Values may be sent and summed in bfloat16 or wider, within the bound.
A program may use at most 128 MiB of HBM per device.

v0:
```python
import jax
import jax.numpy as jnp
from jax import lax
from jax.sharding import PartitionSpec as P


def passed_along(block, axis, distance):
    devices = range(lax.axis_size(axis))
    route = [(i - distance, i) for i in devices if i - distance in devices]
    return lax.ppermute(block, axis, route)


def silu_slope(value):
    sig = jax.nn.sigmoid(value)
    return sig * (1.0 + value * (1.0 - sig))


def conv_back(weights, padded, count):
    taps = weights.shape[0]
    return sum(
        (weights[k][None, :] * padded[taps - 1 - k : taps - 1 - k + count] for k in range(taps))
    )


def on_device(tokens, w_gate, w_conv_in, conv_weight, conv_bias, score_head, targets, loss_mask):
    rows = tokens.shape[0]
    chans = w_gate.shape[1]
    taps = conv_weight.shape[0]
    piece = lax.all_gather(tokens, "tp", axis=1, tiled=True)
    gate_acc = jnp.dot(piece, w_gate, preferred_element_type=jnp.float32)
    xin_acc = jnp.dot(piece, w_conv_in, preferred_element_type=jnp.float32)
    gate16 = lax.optimization_barrier(gate_acc.astype(jnp.bfloat16))
    zgate = gate16.astype(jnp.float32)
    xin16 = lax.optimization_barrier(xin_acc.astype(jnp.bfloat16))
    before = passed_along(xin16[rows - (taps - 1) :], "seq", 1)
    padded = jnp.concatenate([before, xin16], axis=0).astype(jnp.float32)
    conv_out = conv_bias[None, :] + sum(
        (conv_weight[k][None, :] * padded[k : k + rows] for k in range(taps))
    )
    active = jax.nn.silu(conv_out)
    sgate = jax.nn.silu(zgate)
    gated = (active * sgate).astype(jnp.bfloat16)
    scores = score_head.shape[0]
    onehot = (targets[:, None] == jnp.arange(scores, dtype=jnp.int32)[None, :]).astype(jnp.bfloat16)
    picked = jnp.dot(onehot, score_head, preferred_element_type=jnp.float32)
    dgated = loss_mask.astype(jnp.float32)[:, None] * picked
    dgate16 = (dgated * active * silu_slope(zgate)).astype(jnp.bfloat16)
    dconv = dgated * sgate * silu_slope(conv_out)
    edge_zeros = jnp.zeros((taps - 1, chans), jnp.float32)
    local = conv_back(conv_weight, jnp.concatenate([dconv, edge_zeros], axis=0), rows)
    front = conv_back(
        conv_weight, jnp.concatenate([edge_zeros, dconv[: taps - 1]], axis=0), taps - 1
    )
    arrived = passed_along(front, "seq", -1)
    dxin = jnp.concatenate(
        [local[: rows - (taps - 1)], local[rows - (taps - 1) :] + arrived], axis=0
    )
    dxin16 = dxin.astype(jnp.bfloat16)
    spec = (((1,), (1,)), ((), ()))
    terms = lax.dot_general(dgate16, w_gate, spec, preferred_element_type=jnp.float32)
    terms = terms + lax.dot_general(dxin16, w_conv_in, spec, preferred_element_type=jnp.float32)
    d_tokens = lax.psum_scatter(terms.astype(jnp.bfloat16), "tp", scatter_dimension=1, tiled=True)
    return (gated, d_tokens)


def solution(mesh):
    placed = (
        P("seq", "tp"),
        P(None, "tp"),
        P(None, "tp"),
        P(None, "tp"),
        P("tp"),
        P(None, "tp"),
        P("seq"),
        P("seq"),
    )
    return jax.shard_map(
        on_device,
        mesh=mesh,
        in_specs=placed,
        out_specs=(P("seq", "tp"), P("seq", "tp")),
        check_vma=False,
    )
```

profile of v0, /device:TPU:0, one launch (start us, length us, event | category | flops | bytes accessed | tf_op | source)
XLA Modules:
  0.0 180.1 jit_solution(2917227718827997124)
XLA Ops:
  7.2 0.0 copy-start
  7.2 0.0 all-gather.2.cloned.1.call-start
  7.2 0.7 all-gather.2.cloned.1.call-update
  7.9 0.0 reduce-scatter.2.cloned.1.call-start
  8.0 0.7 convert_element_type.31
  8.6 0.9 fusion.31
  9.6 48.7 %all-gather.2.cloned.1.call-done = bf16[128,8192]{1,0:T(8,128)(2,1)} async-done(((bf16[128,2048]{1,0:T(8,128)(2,1)}), bf16[128,8192]{1,0:T(8,128)(2,1)}) %all-gather.2.cloned.1.call-update) | async-done | bytes 2097168 | tf_op jit(solution)/shard_map/all_gather | solution.py:29
  58.3 15.8 %convolution_convert_fusion.1 = bf16[128,2048]{1,0:T(8,128)(2,1)S(1)} fusion(bf16[128,8192]{1,0:T(8,128)(2,1)} %all-gather.2.cloned.1.call-done, bf16[8192,2048]{1,0:T(8,128)(2,1)} %param.10), kind=kOutput, calls=%fused_computation.4 | convolution fusion | flops 4295229440 | bytes 36175872 | tf_op jit(solution)/shard_map/dot_general | solution.py:31
  74.1 0.0 copy-start.3
  74.1 0.0 copy-start.4
  74.1 1.7 collective-permute-start
  75.8 13.0 %convolution_convert_fusion = bf16[128,2048]{1,0:T(8,128)(2,1)S(1)} fusion(bf16[128,8192]{1,0:T(8,128)(2,1)S(1)} %copy-done.2, bf16[8192,2048]{1,0:T(8,128)(2,1)} %param.9), kind=kOutput, calls=%fused_computation.3 | convolution fusion | flops 4295229440 | bytes 36175872 | tf_op jit(solution)/shard_map/dot_general | solution.py:30
  88.9 0.0 collective-permute-done
  88.9 0.1 maximum_convert_fusion
  89.1 1.2 multiply_multiply_fusion
  90.4 1.5 collective-permute-start.1
  91.8 17.2 %fusion.14 = f32[128,8192]{1,0:T(8,128)} fusion(bf16[8192,2048]{1,0:T(8,128)(2,1)} %param.9, bf16[128,2048]{1,0:T(8,128)(2,1)S(1)} %convolution_convert_fusion, f32[128,2048]{1,0:T(8,128)S(1)} %get-tuple-element.8, f32[128,2048]{1,0:T(8,128)S(1)} %get-tuple-element.3), kind=kOutput, calls=%fused_computation.32 | convolution fusion | flops 4298899456 | bytes 40370176 | tf_op jit(solution)/shard_map/dot_general | solution.py:60
  109.0 0.4 multiply_add_fusion
  109.5 0.1 slice.128
  109.6 0.0 copy-start.1
  109.6 18.4 %fusion = bf16[128,8192]{1,0:T(8,128)(2,1)} fusion(f32[128,8192]{1,0:T(8,128)} %fusion.14, bf16[8192,2048]{1,0:T(8,128)(2,1)} %param.10, bf16[3,2048]{1,0:T(4,128)(2,1)S(1)} %fusion.26, bf16[125,2048]{1,0:T(8,128)(2,1)S(1)} %slice.128), kind=kOutput, calls=%fused_computation.1 | convolution fusion | flops 4298113024 | bytes 40370176 | tf_op jit(solution)/shard_map/dot_general | solution.py:61
  128.0 0.0 reduce-scatter.2.cloned.1.call-update
  128.0 1.4 multiply_convert_fusion
  129.4 43.9 %reduce-scatter.2.cloned.1.call-done = bf16[128,2048]{1,0:T(8,128)(2,1)} async-done(((bf16[128,8192]{1,0:T(8,128)(2,1)}), bf16[128,2048]{1,0:T(8,128)(2,1)}) %reduce-scatter.2.cloned.1.call-update) | async-done | bytes 524304 | tf_op jit(solution)/shard_map/reduce_scatter | solution.py:62
  (12 shorter events, 0.1 us)
Async XLA Ops:
  7.2 81.9 %copy-start = (bf16[10,2048]{1,0:T(8,128)(2,1)S(1)}, bf16[10,2048]{1,0:T(8,128)(2,1)}, u32[]{:S(2)}) copy-start(bf16[10,2048]{1,0:T(8,128)(2,1)} %param.13) | copy-start | bytes 122884
  7.2 51.1 %all-gather.2.cloned.1.call-start = ((), (), s32[]{:S(2)}) async-start(), calls=%async_computation.1 | async-start | bytes 2621440 | tf_op jit(solution)/shard_map/all_gather | solution.py:29
  7.9 165.4 %reduce-scatter.2.cloned.1.call-start = ((), (), s32[]{:S(2)}) async-start(), calls=%async_computation.2 | async-start | bytes 2621440 | tf_op jit(solution)/shard_map/reduce_scatter | solution.py:62
  58.3 17.6 %copy-start.2 = (bf16[128,8192]{1,0:T(8,128)(2,1)S(1)}, bf16[128,8192]{1,0:T(8,128)(2,1)}, u32[]{:S(2)}) copy-start(bf16[128,8192]{1,0:T(8,128)(2,1)} %all-gather.2.cloned.1.call-done) | copy-start | bytes 6291460
  74.1 14.9 %copy-start.3 = (f32[2048]{0:T(1024)S(1)}, f32[2048]{0:T(1024)}, u32[]{:S(2)}) copy-start(f32[2048]{0:T(1024)} %param.12) | copy-start | bytes 24580
  74.1 14.9 %copy-start.4 = (s32[128]{0:T(128)S(1)}, s32[128]{0:T(128)}, u32[]{:S(2)}) copy-start(s32[128]{0:T(128)} %param.14) | copy-start | bytes 1540
  74.1 14.7 %collective-permute-start = (bf16[3,2048]{1,0:T(4,128)(2,1)S(1)}, bf16[3,2048]{1,0:T(4,128)(2,1)S(1)}, u32[]{:S(2)}, u32[]{:S(2)}) collective-permute-start(bf16[3,2048]{1,0:T(4,128)(2,1)S(1)} %slice.77), channel_id=1, source_target_pairs={{0,4},{4,8},{8,12},{12,16},{16,20},{20,24},{24,28},{1,5},{5,9},{9,... | collective-permute-start | bytes 36872 | tf_op jit(solution)/shard_map/ppermute | solution.py:10
  90.4 19.2 %collective-permute-start.1 = (f32[3,2048]{1,0:T(4,128)S(1)}, f32[3,2048]{1,0:T(4,128)S(1)}, u32[]{:S(2)}, u32[]{:S(2)}) collective-permute-start(f32[3,2048]{1,0:T(4,128)S(1)} %fusion.24), channel_id=1, source_target_pairs={{4,0},{8,4},{12,8},{16,12},{20,16},{24,20},{28,24},{5,1},{9,5},{13... | collective-permute-start | bytes 73736 | tf_op jit(solution)/shard_map/ppermute | solution.py:10
  109.6 63.7 %copy-start.1 = (bf16[10,2048]{1,0:T(8,128)(2,1)S(1)}, bf16[10,2048]{1,0:T(8,128)(2,1)}, u32[]{:S(2)}) copy-start(bf16[10,2048]{1,0:T(8,128)(2,1)} %param.13) | copy-start | bytes 122884
Sparse Core Ops, SparseCore 0:
  9.6 48.6 all-gather.1
  128.1 45.1 reduce-scatter.1
where the time goes:
time: 181 us; the launch traced here: 180 us
  waiting for transfers between devices  93.3 us (52%)
  matrix products  65.6 us (36%)
  between operations  14.2 us (8%)
  starting transfers between devices  3.25 us (2%)
  other arithmetic  2.67 us (1%)
    all_gather x1, waiting for transfers between devices, on_device(): piece = lax.all_gather(tokens, 'tp', axis=1, tiled=True)  48.7 us
    reduce_scatter x1, waiting for transfers between devices, on_device(): lax.psum_scatter(terms.astype(jnp.bfloat16), 'tp', scatter_dimension=1, t...  43.9 us
    dot_general x1, matrix products, on_device(): lax.dot_general(dxin16, w_conv_in, spec, preferred_element_type=jnp.float32)  18.4 us
    dot_general x1, matrix products, on_device(): lax.dot_general(dgate16, w_gate, spec, preferred_element_type=jnp.float32)  17.2 us
    dot_general x1, matrix products, on_device(): xin_acc = jnp.dot(piece, w_conv_in, preferred_element_type=jnp.float32)  15.8 us
    dot_general x1, matrix products, on_device(): gate_acc = jnp.dot(piece, w_gate, preferred_element_type=jnp.float32)  13 us
  transfers between devices with their start and end apart: 4, of which 2 were waited for; matrix products, arithmetic and copies ran while one was open for 19% of the time, Pallas kernels for 0%

commit v1 on v0

v1 whole, which is shorter than its diff:
```python
import functools

import jax
import jax.numpy as jnp
from jax import lax
from jax.experimental import pallas as pl
from jax.experimental.pallas import tpu as pltpu
from jax.sharding import PartitionSpec as P

MESH = pl.DeviceIdType.MESH
EDGE = 16
LANES = 128


def mixer_kernel(
    n, n_seq, pieces, pc,
    tokens, wg, wc, cw, cb, sh, oh,
    gated, dtok,
    tok, w, acc, zx, grad, part, pair_in, chain_out, chain_in, gbuf, ohx,
    w_sem, own_sem, up_sem, down_sem, z_recv, pair_sem, pair_recv,
    bp_sem, bp_recv, c_sem, c_recv, out_sem, misc,
):
    rows = tokens.shape[0]
    both = 2 * rows
    ext = both + 2 * EDGE
    cols = acc.shape[1]
    half = cols // 2
    taps = cw.shape[0]
    s, z = lax.axis_index("seq"), lax.axis_index("tp")
    core, chip = lax.rem(s, 2), lax.div(s, 2)
    partner = s + 1 - 2 * core
    ahead, behind = lax.rem(s + 2, n_seq), lax.rem(s + n_seq - 2, n_seq)
    has_low, has_high = z > 0, z < n - 1
    mine = pl.ds(pl.multiple_of(core * rows, rows), rows)
    other = pl.ds(pl.multiple_of((1 - core) * rows, rows), rows)
    my_cols = pl.ds(pl.multiple_of(core * half, half), half)

    def remote(src, dst, send, recv, to):
        return pltpu.make_async_remote_copy(
            src_ref=src, dst_ref=dst, send_sem=send, recv_sem=recv, device_id=to, device_id_type=MESH
        )

    def w_copies(j, p):
        r = pl.ds(pl.multiple_of((j * pieces + p) * pc, pc), pc)
        at = j * pieces + p
        return (
            pltpu.make_async_copy(wg.at[r, my_cols], w.at[at, :, pl.ds(0, half)], w_sem.at[at, 0]),
            pltpu.make_async_copy(wc.at[r, my_cols], w.at[at, :, pl.ds(half, half)], w_sem.at[at, 1]),
        )

    def start_w(j, p):
        for copy in w_copies(j, p):
            copy.start()

    def own_src(p):
        return tokens.at[:, pl.ds(p * pc, pc)]

    def slot(j, p):
        return tok.at[j, p, mine, :]

    def own_copy(p):
        return pltpu.make_async_copy(own_src(p), slot(z, p), own_sem.at[p])

    def up_copy(src, j, p):
        return remote(src, slot(j, p), up_sem.at[j, p], z_recv.at[j, p], (s, z + 1))

    def down_copy(src, j, p):
        return remote(src, slot(j, p), down_sem.at[j, p], z_recv.at[j, p], (s, z - 1))

    def pair_copy(src, j, p):
        return remote(src, slot(j, p), pair_sem.at[j, p], pair_recv.at[j, p], (partner, z))

    oh_mine = ohx.at[pl.ds(pl.multiple_of(EDGE + core * rows, EDGE), rows), :]
    oh_local = pltpu.make_async_copy(oh, oh_mine, misc.at[0])
    oh_pair = remote(oh, oh_mine, misc.at[1], misc.at[2], (partner, z))
    oh_edge = remote(
        ohx.at[pl.ds(EDGE, EDGE), :], ohx.at[pl.ds(EDGE + both, EDGE), :], misc.at[3], misc.at[4], (behind, z)
    )
    to_ahead = remote(
        zx.at[pl.ds(both, EDGE), :], zx.at[pl.ds(0, EDGE), :], misc.at[5], misc.at[6], (ahead, z)
    )
    to_behind = remote(
        zx.at[pl.ds(EDGE, EDGE), :], zx.at[pl.ds(EDGE + both, EDGE), :], misc.at[7], misc.at[8], (behind, z)
    )
    g_local = pltpu.make_async_copy(gbuf.at[mine, :], gated.at[:, my_cols], misc.at[9])
    g_pair = remote(gbuf.at[other, :], gated.at[:, my_cols], misc.at[10], misc.at[11], (partner, z))

    for p in range(pieces):
        own_copy(p).start()
    oh_local.start()
    for p in range(pieces):
        start_w(z, p)

    barrier = pltpu.get_barrier_semaphore()
    for to in (partner, ahead, behind):
        pl.semaphore_signal(barrier, inc=1, device_id=(to, z), device_id_type=MESH)

    @pl.when(has_low)
    def _():
        pl.semaphore_signal(barrier, inc=1, device_id=(s, z - 1), device_id_type=MESH)

    @pl.when(has_high)
    def _():
        pl.semaphore_signal(barrier, inc=1, device_id=(s, z + 1), device_id_type=MESH)

    pl.semaphore_wait(barrier, 3 + has_low.astype(jnp.int32) + has_high.astype(jnp.int32))

    for p in range(pieces):
        @pl.when(has_low)
        def _(p=p):
            down_copy(own_src(p), z, p).start()

        @pl.when(has_high)
        def _(p=p):
            up_copy(own_src(p), z, p).start()

        pair_copy(own_src(p), z, p).start()
    oh_pair.start()

    @pl.loop(1, n)
    def _(k):
        for p in range(pieces):
            @pl.when(z - k >= 0)
            def _():
                start_w(z - k, p)

            @pl.when(z + k < n)
            def _():
                start_w(z + k, p)

    ft = min(512, cols)

    def forward(j, p, first=False):
        for copy in w_copies(j, p):
            copy.wait()

        @pl.loop(0, cols // ft)
        def _(t):
            at = pl.ds(pl.multiple_of(t * ft, ft), ft)
            prod = jnp.dot(tok[j, p], w[j * pieces + p, :, at], preferred_element_type=jnp.float32)
            if first:
                acc[:, at] = prod
            else:
                acc[:, at] += prod

    for p in range(pieces):
        own_copy(p).wait()
        pair_copy(own_src(p), z, p).wait_recv()
        forward(z, p, p == 0)

    ohx[pl.ds(0, EDGE), :] = jnp.zeros((EDGE, LANES), ohx.dtype)
    oh_local.wait()
    oh_pair.wait_recv()
    oh_edge.start()

    @pl.loop(1, n)
    def _(k):
        for p in range(pieces):
            low, high = z - k, z + k

            @pl.when(low >= 0)
            def _():
                up_copy(slot(low, p), low, p).wait_recv()

                @pl.when(has_high)
                def _():
                    up_copy(slot(low, p), low, p).start()

                pair_copy(slot(low, p), low, p).start()

            @pl.when(high < n)
            def _():
                down_copy(slot(high, p), high, p).wait_recv()

                @pl.when(has_low)
                def _():
                    down_copy(slot(high, p), high, p).start()

                pair_copy(slot(high, p), high, p).start()

            @pl.when(low >= 0)
            def _():
                pair_copy(slot(low, p), low, p).wait_recv()
                forward(low, p)

            @pl.when(high < n)
            def _():
                pair_copy(slot(high, p), high, p).wait_recv()
                forward(high, p)

    zx[pl.ds(both, EDGE), :] = acc[pl.ds(both - EDGE, EDGE), :].astype(zx.dtype)
    to_ahead.start()
    zx[pl.ds(EDGE, EDGE), :] = acc[pl.ds(0, EDGE), :].astype(zx.dtype)
    to_behind.start()

    @pl.loop(0, (both - 2 * EDGE) // EDGE)
    def _(t):
        r = pl.multiple_of(t * EDGE, EDGE)
        zx[pl.ds(r + 2 * EDGE, EDGE), :] = acc[pl.ds(r + EDGE, EDGE), :].astype(zx.dtype)

    oh_edge.wait_recv()
    to_ahead.wait_recv()
    to_behind.wait_recv()

    ct = min(LANES, half)

    @pl.loop(0, half // ct)
    def _(t):
        gcol = pl.ds(pl.multiple_of(t * ct, ct), ct)
        xcol = pl.ds(pl.multiple_of(half + t * ct, ct), ct)
        wcol = pl.ds(pl.multiple_of(core * half + t * ct, ct), ct)
        row = lax.broadcasted_iota(jnp.int32, (ext, ct), 0)
        taps_w = cw[:, wcol]
        x = zx[:, xcol].astype(jnp.float32)
        x = jnp.where(row < jnp.where(chip == 0, EDGE, 0), 0.0, x)
        u = cb[:, wcol] + taps_w[taps - 1][None, :] * x
        for k in range(taps - 1):
            u += taps_w[k][None, :] * pltpu.roll(x, taps - 1 - k, 0)
        zg = zx[:, gcol].astype(jnp.float32)
        dg = jnp.dot(ohx[...], sh[:, wcol], preferred_element_type=jnp.float32)
        last = jnp.where(chip == n_seq // 2 - 1, EDGE + both, ext)
        dg = jnp.where(row >= last, 0.0, dg)
        su, sz = jax.nn.sigmoid(u), jax.nn.sigmoid(zg)
        act, sg = u * su, zg * sz
        gbuf[:, gcol] = (act * sg)[EDGE : EDGE + both].astype(gbuf.dtype)
        dz = dg * act * (sz * (1.0 + zg * (1.0 - sz)))
        grad[:, gcol] = dz[EDGE : EDGE + both].astype(grad.dtype)
        du = dg * sg * (su * (1.0 + u * (1.0 - su)))
        dx = taps_w[taps - 1][None, :] * du
        for k in range(taps - 1):
            dx += taps_w[k][None, :] * pltpu.roll(du, ext - (taps - 1 - k), 0)
        grad[:, xcol] = dx[EDGE : EDGE + both].astype(grad.dtype)

    g_local.start()
    g_pair.start()

    bt = min(256, pc)

    def bp_copy(j, p):
        return remote(part.at[j, p, other, :], pair_in.at[j, p], bp_sem.at[j, p], bp_recv.at[j, p], (partner, z))

    def chain_copy(j, p):
        dst = jnp.where(j > z, z + 1, z - 1)
        at = jnp.where((j < z) & (j == dst), n, j)
        return remote(chain_out.at[j, p], chain_in.at[at, p], c_sem.at[j, p], c_recv.at[at, p], (s, dst))

    def chain_wait(at, p):
        remote(chain_out.at[0, p], chain_in.at[at, p], c_sem.at[0, p], c_recv.at[at, p], (s, z)).wait_recv()

    def out_copy(p):
        return pltpu.make_async_copy(chain_out.at[z, p], dtok.at[:, pl.ds(p * pc, pc)], out_sem.at[p])

    def backward(j, p):
        @pl.loop(0, pc // bt)
        def _(t):
            at = pl.ds(pl.multiple_of(t * bt, bt), bt)
            prod = lax.dot_general(
                grad[...], w[j * pieces + p, at, :], (((1,), (1,)), ((), ())),
                preferred_element_type=jnp.float32,
            )
            part[j, p, :, at] = prod.astype(part.dtype)

        bp_copy(j, p).start()

    def pair_sum(j, p):
        bp_copy(j, p).wait_recv()
        return part[j, p, mine, :].astype(jnp.float32) + pair_in[j, p].astype(jnp.float32)

    def finish(j, p):
        got = jnp.where(j > z, z, n - 1 - z) > 0

        @pl.when(got)
        def _():
            total = pair_sum(j, p)
            chain_wait(j, p)
            chain_out[j, p] = (total + chain_in[j, p].astype(jnp.float32)).astype(chain_out.dtype)

        @pl.when(jnp.logical_not(got))
        def _():
            chain_out[j, p] = pair_sum(j, p).astype(chain_out.dtype)

        chain_copy(j, p).start()

    low_half = z < n // 2

    def order(i):
        k, p = lax.div(i, pieces), lax.rem(i, pieces)
        far = n - 1 - k
        j_up, j_down = far, k
        return (
            p,
            jnp.where(low_half, j_up, j_down),
            jnp.where(low_half, j_up > z, j_down < z),
            jnp.where(low_half, j_down, j_up),
            jnp.where(low_half, j_down < z, j_up > z),
        )

    def compute(i):
        p, ja, va, jb, vb = order(i)

        @pl.when(va)
        def _():
            backward(ja, p)

        @pl.when(vb)
        def _():
            backward(jb, p)

    steps = (n - 1) * pieces
    compute(jnp.int32(0))

    @pl.loop(0, steps)
    def _(i):
        @pl.when(i + 1 < steps)
        def _():
            compute(i + 1)

        p, ja, va, jb, vb = order(i)

        @pl.when(va)
        def _():
            finish(ja, p)

        @pl.when(vb)
        def _():
            finish(jb, p)

    for p in range(pieces):
        backward(z, p)
    for p in range(pieces):
        tmp = acc.at[pl.ds(0, rows), pl.ds(0, pc)]
        tmp[...] = pair_sum(z, p)

        @pl.when(has_low)
        def _(p=p):
            chain_wait(z, p)
            tmp[...] += chain_in[z, p].astype(jnp.float32)

        @pl.when(has_high)
        def _(p=p):
            chain_wait(n, p)
            tmp[...] += chain_in[n, p].astype(jnp.float32)

        chain_out[z, p] = tmp[...].astype(chain_out.dtype)
        out_copy(p).start()

    @pl.loop(0, n)
    def _(j):
        for p in range(pieces):
            @pl.when((j <= z) & has_high)
            def _():
                up_copy(slot(j, p), j, p).wait_send()

            @pl.when((j >= z) & has_low)
            def _():
                down_copy(slot(j, p), j, p).wait_send()

            pair_copy(slot(j, p), j, p).wait_send()
            bp_copy(j, p).wait_send()

            @pl.when(j != z)
            def _():
                chain_copy(j, p).wait_send()

    for copy in (oh_pair, oh_edge, to_ahead, to_behind):
        copy.wait_send()
    g_local.wait()
    g_pair.wait()
    for p in range(pieces):
        out_copy(p).wait()


def on_device(n, n_seq, tokens, w_gate, w_conv_in, conv_weight, conv_bias, score_head, targets, loss_mask):
    rows, block = tokens.shape
    d, chans = w_gate.shape
    pc = min(512, block)
    pieces = block // pc
    bf16, f32 = jnp.bfloat16, jnp.float32
    picks = (targets[:, None] == jnp.arange(LANES, dtype=jnp.int32)[None, :]) & (loss_mask[:, None] > 0)
    heads = jnp.pad(score_head, ((0, LANES - score_head.shape[0]), (0, 0)))
    both = 2 * rows
    dma = pltpu.SemaphoreType.DMA
    vmem = pl.BlockSpec(memory_space=pltpu.VMEM)
    hbm = pl.BlockSpec(memory_space=pl.ANY)
    per = (n, pieces)
    return pl.pallas_call(
        functools.partial(mixer_kernel, n, n_seq, pieces, pc),
        out_shape=(
            jax.ShapeDtypeStruct((rows, chans), bf16),
            jax.ShapeDtypeStruct((rows, block), bf16),
        ),
        in_specs=[hbm, hbm, hbm, vmem, vmem, vmem, vmem],
        out_specs=(hbm, hbm),
        scratch_shapes=[
            pltpu.VMEM(per + (both, pc), bf16),
            pltpu.VMEM((n * pieces, pc, chans), bf16),
            pltpu.VMEM((both, chans), f32),
            pltpu.VMEM((both + 2 * EDGE, chans), bf16),
            pltpu.VMEM((both, chans), bf16),
            pltpu.VMEM(per + (both, pc), bf16),
            pltpu.VMEM(per + (rows, pc), bf16),
            pltpu.VMEM(per + (rows, pc), bf16),
            pltpu.VMEM((n + 1, pieces, rows, pc), bf16),
            pltpu.VMEM((both, chans // 2), bf16),
            pltpu.VMEM((both + 2 * EDGE, LANES), bf16),
            dma((n * pieces, 2)),
            dma((pieces,)),
            dma(per), dma(per), dma(per), dma(per), dma(per),
            dma(per), dma(per), dma(per), dma((n + 1, pieces)),
            dma((pieces,)),
            dma((12,)),
        ],
        compiler_params=pltpu.CompilerParams(
            collective_id=0, has_side_effects=True, vmem_limit_bytes=60 * 1024 * 1024
        ),
        cost_estimate=pl.CostEstimate(
            flops=8 * rows * d * chans, bytes_accessed=2 * d * chans, transcendentals=2 * both * chans
        ),
    )(tokens, w_gate, w_conv_in, conv_weight, conv_bias[None, :], heads, picks.astype(bf16))


def solution(mesh):
    placed = (
        P("seq", "tp"),
        P(None, "tp"),
        P(None, "tp"),
        P(None, "tp"),
        P("tp"),
        P(None, "tp"),
        P("seq"),
        P("seq"),
    )
    return jax.shard_map(
        functools.partial(on_device, mesh.shape["tp"], mesh.shape["seq"]),
        mesh=mesh,
        in_specs=placed,
        out_specs=(P("seq", "tp"), P("seq", "tp")),
        check_vma=False,
    )
```

time: 181 us -> 103 us (0.57)
  the two profiles are of different devices: /device:TPU:0 before, /device:TPU:8 now
where the time goes in v1:
time: 103 us
  Pallas kernels  94.5 us (92%)
  local copies, waits for them, and re-layouts  5.44 us (5%)
  other arithmetic  2.03 us (2%)
    pallas_call x1, Pallas kernels, on_device(): pl.pallas_call(functools.partial(mixer_kernel, n, n_seq, pieces, pc), out...  94.5 us
    unnamed x2, local copies, waits for them, and re-layouts  3.76 us

profile of v1, /device:TPU:8, one launch (start us, length us, event | category | flops | bytes accessed | tf_op | source)
XLA Modules:
  0.0 102.7 jit_solution(15466127018646260269)
XLA Ops:
  0.6 0.7 broadcast_compare_fusion
  1.3 1.4 %fusion.1.oh = bf16[128,128]{1,0:T(8,128)(2,1)} fusion(s32[128]{0:T(128)} %param.14, pred[128]{0:T(512)(128)(4,1)S(1)} %broadcast_compare_fusion), kind=kLoop, calls=%fused_computation.2 | loop fusion | flops 49152 | bytes 33408 | tf_op jit(solution)/shard_map/convert_element_type | solution.py:419
  2.7 1.7 %pad.4.sh = bf16[128,2048]{1,0:T(8,128)(2,1)} pad(bf16[10,2048]{1,0:T(8,128)(2,1)} %param.13, bf16[]{:T(256)} %constant.1.clone.1), padding=0_118x0_0 | pad | bytes 565250 | tf_op jit(solution)/shard_map/jit(_pad)/pad | solution.py:380
  4.3 94.5 %shard_map.95 = (bf16[128,2048]{1,0:T(8,128)(2,1)}, bf16[128,2048]{1,0:T(8,128)(2,1)}) custom-call(bf16[128,2048]{1,0:T(8,128)(2,1)} %tokens.1, bf16[8192,2048]{1,0:T(8,128)(2,1)} %wg.1, bf16[8192,2048]{1,0:T(8,128)(2,1)} %wc.1, f32[4,2048]{1,0:T(4,128)} %cw.1, f32[1,2048]{1,0:T(1,128)} %bitcast.1, bf16[128,2048]{1,0:T(8,128)(2,1)} %pad.4.sh, ...), custom_call_target="tpu_custom_call" | custom-call | flops 17179869184 | bytes 33554432 | tf_op jit(solution)/shard_map/pallas_call | solution.py:386
  98.9 1.9 %copy.12 = bf16[128,2048]{1,0:T(8,128)(2,1)} copy(bf16[128,2048]{1,0:T(8,128)(2,1)} %get-tuple-element.4) | data formatting | bytes 1048576
  100.8 1.9 %copy.13 = bf16[128,2048]{1,0:T(8,128)(2,1)} copy(bf16[128,2048]{1,0:T(8,128)(2,1)} %get-tuple-element.5) | data formatting | bytes 1048576

commit v2 on v0

v2 whole, which is shorter than its diff:
```python
import functools

import jax
import jax.numpy as jnp
from jax import lax
from jax.experimental import pallas as pl
from jax.experimental.pallas import tpu as pltpu
from jax.sharding import PartitionSpec as P

MESH = pl.DeviceIdType.MESH
EDGE = 16
LANES = 128
LEAD = 3


def mixer_kernel(
    n, n_seq, pieces, pc,
    tokens, wg, wc, cw, cb, sh, tg, mk,
    gated, dtok,
    tok_a, tok_b, w, acc, zx, grad, part, pair_in, chain_out, chain_in, gbuf, ohx, heads,
    w_sem, own_sem, up_sem, down_sem, z_recv, pair_sem, pair_recv,
    bp_sem, bp_recv, c_sem, c_recv, out_sem, misc,
):
    rows = tokens.shape[0]
    both = 2 * rows
    hr = rows // 2
    ext = both + 2 * EDGE
    size = (hr + EDGE, hr - EDGE)
    toks = (tok_a, tok_b)
    cols = acc.shape[1]
    half = cols // 2
    taps = cw.shape[0]
    s, z = lax.axis_index("seq"), lax.axis_index("tp")
    core, chip = lax.rem(s, 2), lax.div(s, 2)
    partner = s + 1 - 2 * core
    ahead, behind = lax.rem(s + 2, n_seq), lax.rem(s + n_seq - 2, n_seq)
    has_low, has_high = z > 0, z < n - 1
    mine = pl.ds(pl.multiple_of(core * rows, rows), rows)
    other = pl.ds(pl.multiple_of((1 - core) * rows, rows), rows)
    mine_h = pl.ds(pl.multiple_of(core * hr, hr), hr)
    other_h = pl.ds(pl.multiple_of((1 - core) * hr, hr), hr)
    my_cols = pl.ds(pl.multiple_of(core * half, half), half)

    def remote(src, dst, send, recv, to):
        return pltpu.make_async_remote_copy(
            src_ref=src, dst_ref=dst, send_sem=send, recv_sem=recv, device_id=to, device_id_type=MESH
        )

    def w_copies(j, p):
        r = pl.ds(pl.multiple_of((j * pieces + p) * pc, pc), pc)
        at = j * pieces + p
        return (
            pltpu.make_async_copy(wg.at[r, my_cols], w.at[at, :, pl.ds(0, half)], w_sem.at[at, 0]),
            pltpu.make_async_copy(wc.at[r, my_cols], w.at[at, :, pl.ds(half, half)], w_sem.at[at, 1]),
        )

    def start_w(j, p):
        for copy in w_copies(j, p):
            copy.start()

    def own_src(q, p):
        first = (1 - core) * size[1] if q == 0 else core * size[0]
        return tokens.at[pl.ds(pl.multiple_of(first, EDGE), size[q]), pl.ds(pl.multiple_of(p * pc, pc), pc)]

    def slot(q, j, p):
        return toks[q].at[j, p, pl.ds(pl.multiple_of(core * size[q], EDGE), size[q]), :]

    def own_copy(q, p):
        return pltpu.make_async_copy(own_src(q, p), slot(q, z, p), own_sem.at[q, p])

    def up_copy(src, q, j, p):
        return remote(src, slot(q, j, p), up_sem.at[q, j, p], z_recv.at[q, j, p], (s, z + 1))

    def down_copy(src, q, j, p):
        return remote(src, slot(q, j, p), down_sem.at[q, j, p], z_recv.at[q, j, p], (s, z - 1))

    def pair_copy(src, q, j, p):
        return remote(src, slot(q, j, p), pair_sem.at[q, j, p], pair_recv.at[q, j, p], (partner, z))

    oh_mine = ohx.at[pl.ds(pl.multiple_of(EDGE + core * rows, EDGE), rows), :]
    oh_pair = remote(oh_mine, oh_mine, misc.at[1], misc.at[2], (partner, z))
    oh_edge = remote(
        ohx.at[pl.ds(EDGE, EDGE), :], ohx.at[pl.ds(EDGE + both, EDGE), :], misc.at[3], misc.at[4], (behind, z)
    )
    to_ahead = remote(
        zx.at[pl.ds(both, EDGE), :], zx.at[pl.ds(0, EDGE), :], misc.at[5], misc.at[6], (ahead, z)
    )
    to_behind = remote(
        zx.at[pl.ds(EDGE, EDGE), :], zx.at[pl.ds(EDGE + both, EDGE), :], misc.at[7], misc.at[8], (behind, z)
    )
    g_local = pltpu.make_async_copy(gbuf.at[mine, :], gated.at[:, my_cols], misc.at[9])
    g_pair = remote(gbuf.at[other, :], gated.at[:, my_cols], misc.at[10], misc.at[11], (partner, z))

    for p in range(pieces):
        own_copy(0, p).start()
    for p in range(pieces):
        start_w(z, p)

    barrier = pltpu.get_barrier_semaphore()
    for to in (partner, ahead, behind):
        pl.semaphore_signal(barrier, inc=1, device_id=(to, z), device_id_type=MESH)

    @pl.when(has_low)
    def _():
        pl.semaphore_signal(barrier, inc=1, device_id=(s, z - 1), device_id_type=MESH)

    @pl.when(has_high)
    def _():
        pl.semaphore_signal(barrier, inc=1, device_id=(s, z + 1), device_id_type=MESH)

    pl.semaphore_wait(barrier, 3 + has_low.astype(jnp.int32) + has_high.astype(jnp.int32))

    def send_own(q):
        for p in range(pieces):
            @pl.when(has_low)
            def _(p=p):
                down_copy(own_src(q, p), q, z, p).start()

            @pl.when(has_high)
            def _(p=p):
                up_copy(own_src(q, p), q, z, p).start()

    for p in range(pieces):
        pair_copy(own_src(0, p), 0, z, p).start()
    send_own(0)

    @pl.loop(1, n)
    def _(k):
        for p in range(pieces):
            @pl.when(z - k >= 0)
            def _():
                start_w(z - k, p)

            @pl.when(z + k < n)
            def _():
                start_w(z + k, p)

    for p in range(pieces):
        own_copy(1, p).start()
        pair_copy(own_src(1, p), 1, z, p).start()

    ids = lax.broadcasted_iota(jnp.int32, (LANES, rows), 0)
    picks = jnp.where((ids == tg[...]) & (mk[...] > 0), 1.0, 0.0)
    oh_mine[...] = jnp.transpose(picks).astype(ohx.dtype)
    oh_pair.start()
    ohx[pl.ds(0, EDGE), :] = jnp.zeros((EDGE, LANES), ohx.dtype)
    heads[...] = jnp.zeros_like(heads)
    heads[pl.ds(0, sh.shape[0]), :] = sh[:, my_cols]

    ft = min(512, cols)

    def forward(q, j, p, first=False):
        if q == 0:
            for copy in w_copies(j, p):
                copy.wait()

        @pl.loop(0, cols // ft)
        def _(t):
            at = pl.ds(pl.multiple_of(t * ft, ft), ft)
            prod = jnp.dot(toks[q][j, p], w[j * pieces + p, :, at], preferred_element_type=jnp.float32)
            if q == 0:
                places = ((pl.ds(size[1], 2 * size[0]), prod),)
            else:
                places = (
                    (pl.ds(0, size[1]), prod[: size[1]]),
                    (pl.ds(both - size[1], size[1]), prod[size[1] :]),
                )
            for place, value in places:
                if first:
                    acc[place, at] = value
                else:
                    acc[place, at] += value

    def own_forward(q, p):
        own_copy(q, p).wait()
        pair_copy(own_src(q, p), q, z, p).wait_recv()
        forward(q, z, p, p == 0)

    def gather_step(q, k, p):
        low, high = z - k, z + k

        @pl.when(low >= 0)
        def _():
            up_copy(slot(q, low, p), q, low, p).wait_recv()

            @pl.when(has_high)
            def _():
                up_copy(slot(q, low, p), q, low, p).start()

            pair_copy(slot(q, low, p), q, low, p).start()

        @pl.when(high < n)
        def _():
            down_copy(slot(q, high, p), q, high, p).wait_recv()

            @pl.when(has_low)
            def _():
                down_copy(slot(q, high, p), q, high, p).start()

            pair_copy(slot(q, high, p), q, high, p).start()

        @pl.when(low >= 0)
        def _():
            pair_copy(slot(q, low, p), q, low, p).wait_recv()
            forward(q, low, p)

        @pl.when(high < n)
        def _():
            pair_copy(slot(q, high, p), q, high, p).wait_recv()
            forward(q, high, p)

    for p in range(pieces):
        own_forward(0, p)

    oh_pair.wait_recv()
    oh_edge.start()

    @pl.loop(1, n)
    def _(k):
        @pl.when(k == n - 1)
        def _():
            send_own(1)

        for p in range(pieces):
            gather_step(0, k, p)

            @pl.when(k == 1)
            def _(p=p):
                own_forward(1, p)

    def round_rows(first, count):
        @pl.loop(0, count // EDGE)
        def _(t):
            r = pl.multiple_of(first + t * EDGE, EDGE)
            zx[pl.ds(r + EDGE, EDGE), :] = acc[pl.ds(r, EDGE), :].astype(zx.dtype)

    ct = min(LANES, half)

    def between(q, e0, count, g0):
        span = count + 2 * EDGE
        window = pl.ds(e0, span)

        @pl.loop(0, half // ct)
        def _(t):
            gcol = pl.ds(pl.multiple_of(t * ct, ct), ct)
            xcol = pl.ds(pl.multiple_of(half + t * ct, ct), ct)
            wcol = pl.ds(pl.multiple_of(core * half + t * ct, ct), ct)
            row = lax.broadcasted_iota(jnp.int32, (span, ct), 0)
            taps_w = cw[:, wcol]
            x = zx[window, xcol].astype(jnp.float32)
            if e0 == 0:
                x = jnp.where(row < jnp.where(chip == 0, EDGE, 0), 0.0, x)
            u = cb[:, wcol] + taps_w[taps - 1][None, :] * x
            for k in range(taps - 1):
                u += taps_w[k][None, :] * pltpu.roll(x, taps - 1 - k, 0)
            zg = zx[window, gcol].astype(jnp.float32)
            dg = jnp.dot(ohx[window, :], heads[:, gcol], preferred_element_type=jnp.float32)
            if e0 + span == ext:
                dg = jnp.where(row >= jnp.where(chip == n_seq // 2 - 1, EDGE + count, span), 0.0, dg)
            su, sz = jax.nn.sigmoid(u), jax.nn.sigmoid(zg)
            act, sg = u * su, zg * sz
            gbuf[pl.ds(e0, count), gcol] = (act * sg)[EDGE : EDGE + count].astype(gbuf.dtype)
            dz = dg * act * (sz * (1.0 + zg * (1.0 - sz)))
            grad[q, pl.ds(g0, count), gcol] = dz[EDGE : EDGE + count].astype(grad.dtype)
            du = dg * sg * (su * (1.0 + u * (1.0 - su)))
            dx = taps_w[taps - 1][None, :] * du
            for k in range(taps - 1):
                dx += taps_w[k][None, :] * pltpu.roll(du, span - (taps - 1 - k), 0)
            grad[q, pl.ds(g0, count), xcol] = dx[EDGE : EDGE + count].astype(grad.dtype)

    bt = min(256, pc)

    def bp_copy(q, j, p):
        return remote(
            part.at[q, j, p, other_h, :], pair_in.at[q, j, p], bp_sem.at[q, j, p], bp_recv.at[q, j, p], (partner, z)
        )

    def chain_copy(q, j, p):
        dst = jnp.where(j > z, z + 1, z - 1)
        at = jnp.where((j < z) & (j == dst), n, j)
        return remote(
            chain_out.at[q, j, p], chain_in.at[q, at, p], c_sem.at[q, j, p], c_recv.at[q, at, p], (s, dst)
        )

    def chain_wait(q, at, p):
        remote(
            chain_out.at[q, 0, p], chain_in.at[q, at, p], c_sem.at[q, 0, p], c_recv.at[q, at, p], (s, z)
        ).wait_recv()

    def out_copy(q, p):
        first = (1 - core) * hr if q == 0 else core * hr
        return pltpu.make_async_copy(
            chain_out.at[q, z, p],
            dtok.at[pl.ds(pl.multiple_of(first, hr), hr), pl.ds(p * pc, pc)],
            out_sem.at[q, p],
        )

    def backward(q, j, p):
        @pl.loop(0, pc // bt)
        def _(t):
            at = pl.ds(pl.multiple_of(t * bt, bt), bt)
            prod = lax.dot_general(
                grad[q], w[j * pieces + p, at, :], (((1,), (1,)), ((), ())),
                preferred_element_type=jnp.float32,
            )
            part[q, j, p, :, at] = prod.astype(part.dtype)

        bp_copy(q, j, p).start()

    def pair_sum(q, j, p):
        bp_copy(q, j, p).wait_recv()
        return part[q, j, p, mine_h, :].astype(jnp.float32) + pair_in[q, j, p].astype(jnp.float32)

    def finish_block(q, j, p):
        got = jnp.where(j > z, z, n - 1 - z) > 0

        @pl.when(got)
        def _():
            total = pair_sum(q, j, p)
            chain_wait(q, j, p)
            chain_out[q, j, p] = (total + chain_in[q, j, p].astype(jnp.float32)).astype(chain_out.dtype)

        @pl.when(jnp.logical_not(got))
        def _():
            chain_out[q, j, p] = pair_sum(q, j, p).astype(chain_out.dtype)

        chain_copy(q, j, p).start()

    low_half = z < n // 2

    def for_blocks(i, act):
        k, p = lax.div(i, pieces), lax.rem(i, pieces)
        far = n - 1 - k
        ja, jb = jnp.where(low_half, far, k), jnp.where(low_half, k, far)

        @pl.when(jnp.where(low_half, far > z, k < z))
        def _():
            act(ja, p)

        @pl.when(jnp.where(low_half, k < z, far > z))
        def _():
            act(jb, p)

    def compute(q, i):
        for_blocks(i, functools.partial(backward, q))

    def finish(q, i):
        for_blocks(i, functools.partial(finish_block, q))

    steps = (n - 1) * pieces
    lead = min(LEAD, steps)

    round_rows(size[1], 2 * size[0])
    between(0, hr, rows, 0)
    compute(0, jnp.int32(0))

    def gather_at(i):
        gather_step(1, 1 + lax.div(i, pieces), lax.rem(i, pieces))

    @pl.loop(0, lead)
    def _(i):
        gather_at(i)

    @pl.loop(0, steps - lead)
    def _(i):
        compute(0, i + 1)
        gather_at(i + lead)
        finish(0, i)

    round_rows(both - EDGE, EDGE)
    to_ahead.start()
    round_rows(0, EDGE)
    to_behind.start()
    round_rows(EDGE, size[1] - EDGE)
    round_rows(both - size[1], size[1] - EDGE)

    @pl.loop(steps - lead, steps)
    def _(i):
        @pl.when(i + 1 < steps)
        def _():
            compute(0, i + 1)

        finish(0, i)

    oh_edge.wait_recv()
    to_ahead.wait_recv()
    to_behind.wait_recv()
    between(1, 0, hr, 0)
    between(1, ext - hr - 2 * EDGE, hr, hr)
    compute(1, jnp.int32(0))
    g_local.start()
    g_pair.start()

    @pl.loop(0, steps)
    def _(i):
        @pl.when(i + 1 < steps)
        def _():
            compute(1, i + 1)

        finish(1, i)

    for q in range(2):
        for p in range(pieces):
            backward(q, z, p)
    for q in range(2):
        for p in range(pieces):
            tmp = acc.at[pl.ds(0, hr), pl.ds(0, pc)]
            tmp[...] = pair_sum(q, z, p)

            @pl.when(has_low)
            def _(q=q, p=p, tmp=tmp):
                chain_wait(q, z, p)
                tmp[...] += chain_in[q, z, p].astype(jnp.float32)

            @pl.when(has_high)
            def _(q=q, p=p, tmp=tmp):
                chain_wait(q, n, p)
                tmp[...] += chain_in[q, n, p].astype(jnp.float32)

            chain_out[q, z, p] = tmp[...].astype(chain_out.dtype)
            out_copy(q, p).start()

    @pl.loop(0, n)
    def _(j):
        for q in range(2):
            for p in range(pieces):
                @pl.when((j <= z) & has_high)
                def _():
                    up_copy(slot(q, j, p), q, j, p).wait_send()

                @pl.when((j >= z) & has_low)
                def _():
                    down_copy(slot(q, j, p), q, j, p).wait_send()

                pair_copy(slot(q, j, p), q, j, p).wait_send()
                bp_copy(q, j, p).wait_send()

                @pl.when(j != z)
                def _():
                    chain_copy(q, j, p).wait_send()

    for copy in (oh_pair, oh_edge, to_ahead, to_behind):
        copy.wait_send()
    g_local.wait()
    g_pair.wait()
    for q in range(2):
        for p in range(pieces):
            out_copy(q, p).wait()


def on_device(n, n_seq, tokens, w_gate, w_conv_in, conv_weight, conv_bias, score_head, targets, loss_mask):
    rows, block = tokens.shape
    d, chans = w_gate.shape
    pc = min(512, block)
    pieces = block // pc
    bf16, f32 = jnp.bfloat16, jnp.float32
    hr = rows // 2
    both = 2 * rows
    dma = pltpu.SemaphoreType.DMA
    vmem = pl.BlockSpec(memory_space=pltpu.VMEM)
    hbm = pl.BlockSpec(memory_space=pl.ANY)
    per = (2, n, pieces)
    return pl.pallas_call(
        functools.partial(mixer_kernel, n, n_seq, pieces, pc),
        out_shape=(
            jax.ShapeDtypeStruct((rows, chans), bf16),
            jax.ShapeDtypeStruct((rows, block), bf16),
        ),
        in_specs=[hbm, hbm, hbm, vmem, vmem, vmem, vmem, vmem],
        out_specs=(hbm, hbm),
        scratch_shapes=[
            pltpu.VMEM((n, pieces, 2 * (hr + EDGE), pc), bf16),
            pltpu.VMEM((n, pieces, 2 * (hr - EDGE), pc), bf16),
            pltpu.VMEM((n * pieces, pc, chans), bf16),
            pltpu.VMEM((both, chans), f32),
            pltpu.VMEM((both + 2 * EDGE, chans), bf16),
            pltpu.VMEM((2, rows, chans), bf16),
            pltpu.VMEM(per + (rows, pc), bf16),
            pltpu.VMEM(per + (hr, pc), bf16),
            pltpu.VMEM(per + (hr, pc), bf16),
            pltpu.VMEM((2, n + 1, pieces, hr, pc), bf16),
            pltpu.VMEM((both, chans // 2), bf16),
            pltpu.VMEM((both + 2 * EDGE, LANES), bf16),
            pltpu.VMEM((LANES, chans // 2), bf16),
            dma((n * pieces, 2)),
            dma((2, pieces)),
            dma(per), dma(per), dma(per), dma(per), dma(per),
            dma(per), dma(per), dma(per), dma((2, n + 1, pieces)),
            dma((2, pieces)),
            dma((12,)),
        ],
        compiler_params=pltpu.CompilerParams(
            collective_id=0, has_side_effects=True, vmem_limit_bytes=60 * 1024 * 1024
        ),
        cost_estimate=pl.CostEstimate(
            flops=8 * rows * d * chans, bytes_accessed=2 * d * chans, transcendentals=2 * both * chans
        ),
    )(tokens, w_gate, w_conv_in, conv_weight, conv_bias[None, :], score_head, targets[None, :], loss_mask[None, :])


def solution(mesh):
    placed = (
        P("seq", "tp"),
        P(None, "tp"),
        P(None, "tp"),
        P(None, "tp"),
        P("tp"),
        P(None, "tp"),
        P("seq"),
        P("seq"),
    )
    return jax.shard_map(
        functools.partial(on_device, mesh.shape["tp"], mesh.shape["seq"]),
        mesh=mesh,
        in_specs=placed,
        out_specs=(P("seq", "tp"), P("seq", "tp")),
        check_vma=False,
    )
```

time: 181 us -> 139 us (0.77)
  the two profiles are of different devices: /device:TPU:0 before, /device:TPU:8 now
where the time goes in v2:
time: 139 us; the launch traced here: 137 us
  Pallas kernels  132 us (95%)
  local copies, waits for them, and re-layouts  3.76 us (3%)
    pallas_call x1, Pallas kernels, on_device(): pl.pallas_call(functools.partial(mixer_kernel, n, n_seq, pieces, pc), out...  132 us
    unnamed x2, local copies, waits for them, and re-layouts  3.76 us

profile of v2, /device:TPU:8, one launch (start us, length us, event | category | flops | bytes accessed | tf_op | source)
XLA Modules:
  0.0 136.7 jit_solution(11765977537327253116)
XLA Ops:
  0.6 132.3 %shard_map.95 = (bf16[128,2048]{1,0:T(8,128)(2,1)}, bf16[128,2048]{1,0:T(8,128)(2,1)}) custom-call(bf16[128,2048]{1,0:T(8,128)(2,1)} %tokens.1, bf16[8192,2048]{1,0:T(8,128)(2,1)} %wg.1, bf16[8192,2048]{1,0:T(8,128)(2,1)} %wc.1, f32[4,2048]{1,0:T(4,128)} %cw.1, f32[1,2048]{1,0:T(1,128)} %bitcast.3, bf16[10,2048]{1,0:T(8,128)(2,1)} %sh.1, s32[1,128]{1,0:T(1,128)} %bitcast.4, ...), custom_call_target="tpu_custom_call" | custom-call | flops 17179869184 | bytes 33554432 | tf_op jit(solution)/shard_map/pallas_call | solution.py:463
  132.9 1.9 %copy.12 = bf16[128,2048]{1,0:T(8,128)(2,1)} copy(bf16[128,2048]{1,0:T(8,128)(2,1)} %get-tuple-element.4) | data formatting | bytes 1048576
  134.8 1.9 %copy.13 = bf16[128,2048]{1,0:T(8,128)(2,1)} copy(bf16[128,2048]{1,0:T(8,128)(2,1)} %get-tuple-element.5) | data formatting | bytes 1048576

commit v3 on v2

--- a/solution.py
+++ b/solution.py
@@ -17,7 +17,7 @@
     n, n_seq, pieces, pc,
     tokens, wg, wc, cw, cb, sh, tg, mk,
     gated, dtok,
-    tok_a, tok_b, w, acc, zx, grad, part, pair_in, chain_out, chain_in, gbuf, ohx, heads,
+    tok_a, tok_b, w, acc, zx, grad, part, pair_in, chain_out, chain_in, gbuf, ohx, heads, obuf,
     w_sem, own_sem, up_sem, down_sem, z_recv, pair_sem, pair_recv,
     bp_sem, bp_recv, c_sem, c_recv, out_sem, misc,
 ):
@@ -39,6 +39,8 @@
     other = pl.ds(pl.multiple_of((1 - core) * rows, rows), rows)
     mine_h = pl.ds(pl.multiple_of(core * hr, hr), hr)
     other_h = pl.ds(pl.multiple_of((1 - core) * hr, hr), hr)
+    mine_d = pl.ds(pl.multiple_of(core * (pc // 2), pc // 2), pc // 2)
+    other_d = pl.ds(pl.multiple_of((1 - core) * (pc // 2), pc // 2), pc // 2)
     my_cols = pl.ds(pl.multiple_of(core * half, half), half)
 
     def remote(src, dst, send, recv, to):
@@ -236,43 +238,48 @@
 
     ct = min(LANES, half)
 
-    def between(q, e0, count, g0):
+    def window_values(e0, count, gcol, xcol, wcol, taps_w):
         span = count + 2 * EDGE
         window = pl.ds(e0, span)
-
+        inner = slice(EDGE, EDGE + count)
+        row = lax.broadcasted_iota(jnp.int32, (span, ct), 0)
+        x = zx[window, xcol].astype(jnp.float32)
+        if e0 == 0:
+            x = jnp.where(row < jnp.where(chip == 0, EDGE, 0), 0.0, x)
+        u = cb[:, wcol] + taps_w[taps - 1][None, :] * x
+        for k in range(taps - 1):
+            u += taps_w[k][None, :] * pltpu.roll(x, taps - 1 - k, 0)
+        zg = zx[window, gcol].astype(jnp.float32)
+        dg = jnp.dot(ohx[window, :], heads[:, gcol], preferred_element_type=jnp.float32)
+        if e0 + span == ext:
+            dg = jnp.where(row >= jnp.where(chip == n_seq // 2 - 1, EDGE + count, span), 0.0, dg)
+        su, sz = jax.nn.sigmoid(u), jax.nn.sigmoid(zg)
+        act, sg = u * su, zg * sz
+        gbuf[pl.ds(e0, count), gcol] = (act * sg)[inner].astype(gbuf.dtype)
+        dz = dg * act * (sz * (1.0 + zg * (1.0 - sz)))
+        du = dg * sg * (su * (1.0 + u * (1.0 - su)))
+        dx = taps_w[taps - 1][None, :] * du
+        for k in range(taps - 1):
+            dx += taps_w[k][None, :] * pltpu.roll(du, span - (taps - 1 - k), 0)
+        return dz[inner], dx[inner]
+
+    def between(q, *windows):
         @pl.loop(0, half // ct)
         def _(t):
             gcol = pl.ds(pl.multiple_of(t * ct, ct), ct)
             xcol = pl.ds(pl.multiple_of(half + t * ct, ct), ct)
             wcol = pl.ds(pl.multiple_of(core * half + t * ct, ct), ct)
-            row = lax.broadcasted_iota(jnp.int32, (span, ct), 0)
             taps_w = cw[:, wcol]
-            x = zx[window, xcol].astype(jnp.float32)
-            if e0 == 0:
-                x = jnp.where(row < jnp.where(chip == 0, EDGE, 0), 0.0, x)
-            u = cb[:, wcol] + taps_w[taps - 1][None, :] * x
-            for k in range(taps - 1):
-                u += taps_w[k][None, :] * pltpu.roll(x, taps - 1 - k, 0)
-            zg = zx[window, gcol].astype(jnp.float32)
-            dg = jnp.dot(ohx[window, :], heads[:, gcol], preferred_element_type=jnp.float32)
-            if e0 + span == ext:
-                dg = jnp.where(row >= jnp.where(chip == n_seq // 2 - 1, EDGE + count, span), 0.0, dg)
-            su, sz = jax.nn.sigmoid(u), jax.nn.sigmoid(zg)
-            act, sg = u * su, zg * sz
-            gbuf[pl.ds(e0, count), gcol] = (act * sg)[EDGE : EDGE + count].astype(gbuf.dtype)
-            dz = dg * act * (sz * (1.0 + zg * (1.0 - sz)))
-            grad[q, pl.ds(g0, count), gcol] = dz[EDGE : EDGE + count].astype(grad.dtype)
-            du = dg * sg * (su * (1.0 + u * (1.0 - su)))
-            dx = taps_w[taps - 1][None, :] * du
-            for k in range(taps - 1):
-                dx += taps_w[k][None, :] * pltpu.roll(du, span - (taps - 1 - k), 0)
-            grad[q, pl.ds(g0, count), xcol] = dx[EDGE : EDGE + count].astype(grad.dtype)
-
-    bt = min(256, pc)
+            found = [window_values(e0, count, gcol, xcol, wcol, taps_w) for e0, count in windows]
+            for at, values in ((gcol, [f[0] for f in found]), (xcol, [f[1] for f in found])):
+                value = values[0] if len(values) == 1 else jnp.concatenate(values, axis=0)
+                grad[q, at, :] = jnp.transpose(value).astype(grad.dtype)
+
+    hd = pc // 2
 
     def bp_copy(q, j, p):
         return remote(
-            part.at[q, j, p, other_h, :], pair_in.at[q, j, p], bp_sem.at[q, j, p], bp_recv.at[q, j, p], (partner, z)
+            part.at[q, j, p, other_d, :], pair_in.at[q, j, p], bp_sem.at[q, j, p], bp_recv.at[q, j, p], (partner, z)
         )
 
     def chain_copy(q, j, p):
@@ -287,29 +294,28 @@
             chain_out.at[q, 0, p], chain_in.at[q, at, p], c_sem.at[q, 0, p], c_recv.at[q, at, p], (s, z)
         ).wait_recv()
 
-    def out_copy(q, p):
-        first = (1 - core) * hr if q == 0 else core * hr
-        return pltpu.make_async_copy(
-            chain_out.at[q, z, p],
-            dtok.at[pl.ds(pl.multiple_of(first, hr), hr), pl.ds(p * pc, pc)],
-            out_sem.at[q, p],
+    def out_copies(q, p):
+        def place(to):
+            first = (1 - to) * hr if q == 0 else to * hr
+            return dtok.at[
+                pl.ds(pl.multiple_of(first, hr), hr), pl.ds(pl.multiple_of(p * pc + core * hd, hd), hd)
+            ]
+
+        return (
+            remote(
+                obuf.at[q, p, other_h, :], place(1 - core), out_sem.at[q, p, 0], out_sem.at[q, p, 1], (partner, z)
+            ),
+            pltpu.make_async_copy(obuf.at[q, p, mine_h, :], place(core), out_sem.at[q, p, 2]),
         )
 
     def backward(q, j, p):
-        @pl.loop(0, pc // bt)
-        def _(t):
-            at = pl.ds(pl.multiple_of(t * bt, bt), bt)
-            prod = lax.dot_general(
-                grad[q], w[j * pieces + p, at, :], (((1,), (1,)), ((), ())),
-                preferred_element_type=jnp.float32,
-            )
-            part[q, j, p, :, at] = prod.astype(part.dtype)
-
+        prod = jnp.dot(w[j * pieces + p], grad[q], preferred_element_type=jnp.float32)
+        part[q, j, p] = prod.astype(part.dtype)
         bp_copy(q, j, p).start()
 
     def pair_sum(q, j, p):
         bp_copy(q, j, p).wait_recv()
-        return part[q, j, p, mine_h, :].astype(jnp.float32) + pair_in[q, j, p].astype(jnp.float32)
+        return part[q, j, p, mine_d, :].astype(jnp.float32) + pair_in[q, j, p].astype(jnp.float32)
 
     def finish_block(q, j, p):
         got = jnp.where(j > z, z, n - 1 - z) > 0
@@ -351,7 +357,7 @@
     lead = min(LEAD, steps)
 
     round_rows(size[1], 2 * size[0])
-    between(0, hr, rows, 0)
+    between(0, (hr, rows))
     compute(0, jnp.int32(0))
 
     def gather_at(i):
@@ -385,8 +391,7 @@
     oh_edge.wait_recv()
     to_ahead.wait_recv()
     to_behind.wait_recv()
-    between(1, 0, hr, 0)
-    between(1, ext - hr - 2 * EDGE, hr, hr)
+    between(1, (0, hr), (ext - hr - 2 * EDGE, hr))
     compute(1, jnp.int32(0))
     g_local.start()
     g_pair.start()
@@ -404,7 +409,7 @@
             backward(q, z, p)
     for q in range(2):
         for p in range(pieces):
-            tmp = acc.at[pl.ds(0, hr), pl.ds(0, pc)]
+            tmp = acc.at[pl.ds(0, hd), pl.ds(0, rows)]
             tmp[...] = pair_sum(q, z, p)
 
             @pl.when(has_low)
@@ -417,8 +422,9 @@
                 chain_wait(q, n, p)
                 tmp[...] += chain_in[q, n, p].astype(jnp.float32)
 
-            chain_out[q, z, p] = tmp[...].astype(chain_out.dtype)
-            out_copy(q, p).start()
+            obuf[q, p] = jnp.transpose(tmp[...]).astype(obuf.dtype)
+            for copy in out_copies(q, p):
+                copy.start()
 
     @pl.loop(0, n)
     def _(j):
@@ -445,7 +451,8 @@
     g_pair.wait()
     for q in range(2):
         for p in range(pieces):
-            out_copy(q, p).wait()
+            for copy in out_copies(q, p):
+                copy.wait()
 
 
 def on_device(n, n_seq, tokens, w_gate, w_conv_in, conv_weight, conv_bias, score_head, targets, loss_mask):
@@ -474,19 +481,20 @@
             pltpu.VMEM((n * pieces, pc, chans), bf16),
             pltpu.VMEM((both, chans), f32),
             pltpu.VMEM((both + 2 * EDGE, chans), bf16),
-            pltpu.VMEM((2, rows, chans), bf16),
-            pltpu.VMEM(per + (rows, pc), bf16),
-            pltpu.VMEM(per + (hr, pc), bf16),
-            pltpu.VMEM(per + (hr, pc), bf16),
-            pltpu.VMEM((2, n + 1, pieces, hr, pc), bf16),
+            pltpu.VMEM((2, chans, rows), bf16),
+            pltpu.VMEM(per + (pc, rows), bf16),
+            pltpu.VMEM(per + (pc // 2, rows), bf16),
+            pltpu.VMEM(per + (pc // 2, rows), bf16),
+            pltpu.VMEM((2, n + 1, pieces, pc // 2, rows), bf16),
             pltpu.VMEM((both, chans // 2), bf16),
             pltpu.VMEM((both + 2 * EDGE, LANES), bf16),
             pltpu.VMEM((LANES, chans // 2), bf16),
+            pltpu.VMEM((2, pieces, rows, pc // 2), bf16),
             dma((n * pieces, 2)),
             dma((2, pieces)),
             dma(per), dma(per), dma(per), dma(per), dma(per),
             dma(per), dma(per), dma(per), dma((2, n + 1, pieces)),
-            dma((2, pieces)),
+            dma((2, pieces, 3)),
             dma((12,)),
         ],
         compiler_params=pltpu.CompilerParams(

time: 139 us -> 139 us (level)
  the two profiles are of different devices: /device:TPU:8 before, /device:TPU:19 now
where the time goes in v3:
time: 139 us; the launch traced here: 138 us
  Pallas kernels  134 us (96%)
  local copies, waits for them, and re-layouts  3.76 us (3%)
    pallas_call x1, Pallas kernels, on_device(): pl.pallas_call(functools.partial(mixer_kernel, n, n_seq, pieces, pc), out...  134 us
    unnamed x2, local copies, waits for them, and re-layouts  3.76 us

profile of v3, /device:TPU:19, one launch (start us, length us, event | category | flops | bytes accessed | tf_op | source)
XLA Modules:
  0.0 138.4 jit_solution(16947201918780677)
XLA Ops:
  0.6 134.0 %shard_map.95 = (bf16[128,2048]{1,0:T(8,128)(2,1)}, bf16[128,2048]{1,0:T(8,128)(2,1)}) custom-call(bf16[128,2048]{1,0:T(8,128)(2,1)} %tokens.1, bf16[8192,2048]{1,0:T(8,128)(2,1)} %wg.1, bf16[8192,2048]{1,0:T(8,128)(2,1)} %wc.1, f32[4,2048]{1,0:T(4,128)} %cw.1, f32[1,2048]{1,0:T(1,128)} %bitcast.3, bf16[10,2048]{1,0:T(8,128)(2,1)} %sh.1, s32[1,128]{1,0:T(1,128)} %bitcast.4, ...), custom_call_target="tpu_custom_call" | custom-call | flops 17179869184 | bytes 33554432 | tf_op jit(solution)/shard_map/pallas_call | solution.py:470
  134.6 1.9 %copy.12 = bf16[128,2048]{1,0:T(8,128)(2,1)} copy(bf16[128,2048]{1,0:T(8,128)(2,1)} %get-tuple-element.4) | data formatting | bytes 1048576
  136.5 1.9 %copy.13 = bf16[128,2048]{1,0:T(8,128)(2,1)} copy(bf16[128,2048]{1,0:T(8,128)(2,1)} %get-tuple-element.5) | data formatting | bytes 1048576

commit v4 on v3

--- a/solution.py
+++ b/solution.py
@@ -10,14 +10,14 @@
 MESH = pl.DeviceIdType.MESH
 EDGE = 16
 LANES = 128
-LEAD = 3
+LEAD = 2
 
 
 def mixer_kernel(
     n, n_seq, pieces, pc,
     tokens, wg, wc, cw, cb, sh, tg, mk,
     gated, dtok,
-    tok_a, tok_b, w, acc, zx, grad, part, pair_in, chain_out, chain_in, gbuf, ohx, heads, obuf,
+    tok_a, tok_b, w, acc, zx, grad, part, pair_in, chain_out, chain_in, gbuf, ohx, heads, obuf, tmp,
     w_sem, own_sem, up_sem, down_sem, z_recv, pair_sem, pair_recv,
     bp_sem, bp_recv, c_sem, c_recv, out_sem, misc,
 ):
@@ -201,6 +201,9 @@
 
             pair_copy(slot(q, high, p), q, high, p).start()
 
+    def multiply_step(q, k, p):
+        low, high = z - k, z + k
+
         @pl.when(low >= 0)
         def _():
             pair_copy(slot(q, low, p), q, low, p).wait_recv()
@@ -225,6 +228,7 @@
 
         for p in range(pieces):
             gather_step(0, k, p)
+            multiply_step(0, k, p)
 
             @pl.when(k == 1)
             def _(p=p):
@@ -275,6 +279,7 @@
                 value = values[0] if len(values) == 1 else jnp.concatenate(values, axis=0)
                 grad[q, at, :] = jnp.transpose(value).astype(grad.dtype)
 
+    bt = min(512, pc)
     hd = pc // 2
 
     def bp_copy(q, j, p):
@@ -309,8 +314,12 @@
         )
 
     def backward(q, j, p):
-        prod = jnp.dot(w[j * pieces + p], grad[q], preferred_element_type=jnp.float32)
-        part[q, j, p] = prod.astype(part.dtype)
+        @pl.loop(0, pc // bt)
+        def _(t):
+            at = pl.ds(pl.multiple_of(t * bt, bt), bt)
+            prod = jnp.dot(w[j * pieces + p, at, :], grad[q], preferred_element_type=jnp.float32)
+            part[q, j, p, at, :] = prod.astype(part.dtype)
+
         bp_copy(q, j, p).start()
 
     def pair_sum(q, j, p):
@@ -360,17 +369,19 @@
     between(0, (hr, rows))
     compute(0, jnp.int32(0))
 
-    def gather_at(i):
-        gather_step(1, 1 + lax.div(i, pieces), lax.rem(i, pieces))
+    def at_step(act, i):
+        act(1, 1 + lax.div(i, pieces), lax.rem(i, pieces))
 
     @pl.loop(0, lead)
     def _(i):
-        gather_at(i)
+        at_step(gather_step, i)
+        at_step(multiply_step, i)
 
     @pl.loop(0, steps - lead)
     def _(i):
+        at_step(gather_step, i + lead)
         compute(0, i + 1)
-        gather_at(i + lead)
+        at_step(multiply_step, i + lead)
         finish(0, i)
 
     round_rows(both - EDGE, EDGE)
@@ -388,6 +399,8 @@
 
         finish(0, i)
 
+    for p in range(pieces):
+        backward(0, z, p)
     oh_edge.wait_recv()
     to_ahead.wait_recv()
     to_behind.wait_recv()
@@ -396,6 +409,23 @@
     g_local.start()
     g_pair.start()
 
+    def own_sum(q, p):
+        tmp[...] = pair_sum(q, z, p)
+
+        @pl.when(has_low)
+        def _():
+            chain_wait(q, z, p)
+            tmp[...] += chain_in[q, z, p].astype(jnp.float32)
+
+        @pl.when(has_high)
+        def _():
+            chain_wait(q, n, p)
+            tmp[...] += chain_in[q, n, p].astype(jnp.float32)
+
+        obuf[q, p] = jnp.transpose(tmp[...]).astype(obuf.dtype)
+        for copy in out_copies(q, p):
+            copy.start()
+
     @pl.loop(0, steps)
     def _(i):
         @pl.when(i + 1 < steps)
@@ -404,27 +434,13 @@
 
         finish(1, i)
 
-    for q in range(2):
-        for p in range(pieces):
-            backward(q, z, p)
-    for q in range(2):
-        for p in range(pieces):
-            tmp = acc.at[pl.ds(0, hd), pl.ds(0, rows)]
-            tmp[...] = pair_sum(q, z, p)
-
-            @pl.when(has_low)
-            def _(q=q, p=p, tmp=tmp):
-                chain_wait(q, z, p)
-                tmp[...] += chain_in[q, z, p].astype(jnp.float32)
-
-            @pl.when(has_high)
-            def _(q=q, p=p, tmp=tmp):
-                chain_wait(q, n, p)
-                tmp[...] += chain_in[q, n, p].astype(jnp.float32)
-
-            obuf[q, p] = jnp.transpose(tmp[...]).astype(obuf.dtype)
-            for copy in out_copies(q, p):
-                copy.start()
+        @pl.when(i >= steps - pieces)
+        def _():
+            own_sum(0, i - (steps - pieces))
+            backward(1, z, i - (steps - pieces))
+
+    for p in range(pieces):
+        own_sum(1, p)
 
     @pl.loop(0, n)
     def _(j):
@@ -458,7 +474,7 @@
 def on_device(n, n_seq, tokens, w_gate, w_conv_in, conv_weight, conv_bias, score_head, targets, loss_mask):
     rows, block = tokens.shape
     d, chans = w_gate.shape
-    pc = min(512, block)
+    pc = min(1024, block)
     pieces = block // pc
     bf16, f32 = jnp.bfloat16, jnp.float32
     hr = rows // 2
@@ -490,6 +506,7 @@
             pltpu.VMEM((both + 2 * EDGE, LANES), bf16),
             pltpu.VMEM((LANES, chans // 2), bf16),
             pltpu.VMEM((2, pieces, rows, pc // 2), bf16),
+            pltpu.VMEM((pc // 2, rows), f32),
             dma((n * pieces, 2)),
             dma((2, pieces)),
             dma(per), dma(per), dma(per), dma(per), dma(per),

time: 139 us -> 105 us (0.76)
  the two profiles are of different devices: /device:TPU:19 before, /device:TPU:8 now
where the time goes in v4:
time: 105 us; the launch traced here: 104 us
  Pallas kernels  99.4 us (95%)
  local copies, waits for them, and re-layouts  3.76 us (4%)
    pallas_call x1, Pallas kernels, on_device(): pl.pallas_call(functools.partial(mixer_kernel, n, n_seq, pieces, pc), out...  99.4 us
    unnamed x2, local copies, waits for them, and re-layouts  3.76 us

profile of v4, /device:TPU:8, one launch (start us, length us, event | category | flops | bytes accessed | tf_op | source)
XLA Modules:
  0.0 103.8 jit_solution(9007458632601700143)
XLA Ops:
  0.6 99.4 %shard_map.95 = (bf16[128,2048]{1,0:T(8,128)(2,1)}, bf16[128,2048]{1,0:T(8,128)(2,1)}) custom-call(bf16[128,2048]{1,0:T(8,128)(2,1)} %tokens.1, bf16[8192,2048]{1,0:T(8,128)(2,1)} %wg.1, bf16[8192,2048]{1,0:T(8,128)(2,1)} %wc.1, f32[4,2048]{1,0:T(4,128)} %cw.1, f32[1,2048]{1,0:T(1,128)} %bitcast.3, bf16[10,2048]{1,0:T(8,128)(2,1)} %sh.1, s32[1,128]{1,0:T(1,128)} %bitcast.4, ...), custom_call_target="tpu_custom_call" | custom-call | flops 17179869184 | bytes 33554432 | tf_op jit(solution)/shard_map/pallas_call | solution.py:486
  100.0 1.9 %copy.12 = bf16[128,2048]{1,0:T(8,128)(2,1)} copy(bf16[128,2048]{1,0:T(8,128)(2,1)} %get-tuple-element.4) | data formatting | bytes 1048576
  101.9 1.9 %copy.13 = bf16[128,2048]{1,0:T(8,128)(2,1)} copy(bf16[128,2048]{1,0:T(8,128)(2,1)} %get-tuple-element.5) | data formatting | bytes 1048576

commit v5 on v4

--- a/solution.py
+++ b/solution.py
@@ -10,7 +10,7 @@
 MESH = pl.DeviceIdType.MESH
 EDGE = 16
 LANES = 128
-LEAD = 2
+LEAD = 1
 
 
 def mixer_kernel(
@@ -474,7 +474,7 @@
 def on_device(n, n_seq, tokens, w_gate, w_conv_in, conv_weight, conv_bias, score_head, targets, loss_mask):
     rows, block = tokens.shape
     d, chans = w_gate.shape
-    pc = min(1024, block)
+    pc = min(2048, block)
     pieces = block // pc
     bf16, f32 = jnp.bfloat16, jnp.float32
     hr = rows // 2

time: 105 us -> 95.2 us (0.907)
  Pallas kernels: 99.4 us -> 89.8 us
    pallas_call x1, Pallas kernels: 99.4 us -> 89.8 us  [on_device(): pl.pallas_call(functools.partial(mixer_kernel, n, n_seq, pieces, pc), out...]
where the time goes in v5:
time: 95.2 us; the launch traced here: 94.2 us
  Pallas kernels  89.8 us (94%)
  local copies, waits for them, and re-layouts  3.76 us (4%)
    pallas_call x1, Pallas kernels, on_device(): pl.pallas_call(functools.partial(mixer_kernel, n, n_seq, pieces, pc), out...  89.8 us
    unnamed x2, local copies, waits for them, and re-layouts  3.76 us

profile of v5, /device:TPU:8, one launch (start us, length us, event | category | flops | bytes accessed | tf_op | source)
XLA Modules:
  0.0 94.2 jit_solution(11914934906133344645)
XLA Ops:
  0.6 89.8 %shard_map.95 = (bf16[128,2048]{1,0:T(8,128)(2,1)}, bf16[128,2048]{1,0:T(8,128)(2,1)}) custom-call(bf16[128,2048]{1,0:T(8,128)(2,1)} %tokens.1, bf16[8192,2048]{1,0:T(8,128)(2,1)} %wg.1, bf16[8192,2048]{1,0:T(8,128)(2,1)} %wc.1, f32[4,2048]{1,0:T(4,128)} %cw.1, f32[1,2048]{1,0:T(1,128)} %bitcast.3, bf16[10,2048]{1,0:T(8,128)(2,1)} %sh.1, s32[1,128]{1,0:T(1,128)} %bitcast.4, ...), custom_call_target="tpu_custom_call" | custom-call | flops 17179869184 | bytes 33554432 | tf_op jit(solution)/shard_map/pallas_call | solution.py:486
  90.4 1.9 %copy.12 = bf16[128,2048]{1,0:T(8,128)(2,1)} copy(bf16[128,2048]{1,0:T(8,128)(2,1)} %get-tuple-element.4) | data formatting | bytes 1048576
  92.3 1.9 %copy.13 = bf16[128,2048]{1,0:T(8,128)(2,1)} copy(bf16[128,2048]{1,0:T(8,128)(2,1)} %get-tuple-element.5) | data formatting | bytes 1048576

commit v6 on v5

--- a/solution.py
+++ b/solution.py
@@ -10,7 +10,6 @@
 MESH = pl.DeviceIdType.MESH
 EDGE = 16
 LANES = 128
-LEAD = 1
 
 
 def mixer_kernel(
@@ -267,13 +266,15 @@
             dx += taps_w[k][None, :] * pltpu.roll(du, span - (taps - 1 - k), 0)
         return dz[inner], dx[inner]
 
-    def between(q, *windows):
+    def between(q, *windows, midway=None):
         @pl.loop(0, half // ct)
         def _(t):
             gcol = pl.ds(pl.multiple_of(t * ct, ct), ct)
             xcol = pl.ds(pl.multiple_of(half + t * ct, ct), ct)
             wcol = pl.ds(pl.multiple_of(core * half + t * ct, ct), ct)
             taps_w = cw[:, wcol]
+            if midway is not None:
+                pl.when(t == half // ct // 2)(midway)
             found = [window_values(e0, count, gcol, xcol, wcol, taps_w) for e0, count in windows]
             for at, values in ((gcol, [f[0] for f in found]), (xcol, [f[1] for f in found])):
                 value = values[0] if len(values) == 1 else jnp.concatenate(values, axis=0)
@@ -326,20 +327,22 @@
         bp_copy(q, j, p).wait_recv()
         return part[q, j, p, mine_d, :].astype(jnp.float32) + pair_in[q, j, p].astype(jnp.float32)
 
+    def has_chain(j):
+        return jnp.where(j > z, z, n - 1 - z) > 0
+
+    def launch_block(q, j, p):
+        @pl.when(jnp.logical_not(has_chain(j)))
+        def _():
+            chain_out[q, j, p] = pair_sum(q, j, p).astype(chain_out.dtype)
+            chain_copy(q, j, p).start()
+
     def finish_block(q, j, p):
-        got = jnp.where(j > z, z, n - 1 - z) > 0
-
-        @pl.when(got)
+        @pl.when(has_chain(j))
         def _():
             total = pair_sum(q, j, p)
             chain_wait(q, j, p)
             chain_out[q, j, p] = (total + chain_in[q, j, p].astype(jnp.float32)).astype(chain_out.dtype)
-
-        @pl.when(jnp.logical_not(got))
-        def _():
-            chain_out[q, j, p] = pair_sum(q, j, p).astype(chain_out.dtype)
-
-        chain_copy(q, j, p).start()
+            chain_copy(q, j, p).start()
 
     low_half = z < n // 2
 
@@ -358,31 +361,30 @@
 
     def compute(q, i):
         for_blocks(i, functools.partial(backward, q))
+        for_blocks(i, functools.partial(launch_block, q))
 
     def finish(q, i):
         for_blocks(i, functools.partial(finish_block, q))
 
     steps = (n - 1) * pieces
-    lead = min(LEAD, steps)
-
-    round_rows(size[1], 2 * size[0])
-    between(0, (hr, rows))
-    compute(0, jnp.int32(0))
 
     def at_step(act, i):
         act(1, 1 + lax.div(i, pieces), lax.rem(i, pieces))
 
-    @pl.loop(0, lead)
+    round_rows(size[1], 2 * size[0])
+    between(0, (hr, rows), midway=lambda: at_step(gather_step, jnp.int32(0)))
+    compute(0, jnp.int32(0))
+    at_step(multiply_step, jnp.int32(0))
+
+    @pl.loop(0, steps - 1)
     def _(i):
-        at_step(gather_step, i)
-        at_step(multiply_step, i)
-
-    @pl.loop(0, steps - lead)
-    def _(i):
-        at_step(gather_step, i + lead)
+        @pl.when(i > 0)
+        def _():
+            finish(0, i - 1)
+
+        at_step(gather_step, i + 1)
         compute(0, i + 1)
-        at_step(multiply_step, i + lead)
-        finish(0, i)
+        at_step(multiply_step, i + 1)
 
     round_rows(both - EDGE, EDGE)
     to_ahead.start()
@@ -391,12 +393,8 @@
     round_rows(EDGE, size[1] - EDGE)
     round_rows(both - size[1], size[1] - EDGE)
 
-    @pl.loop(steps - lead, steps)
+    @pl.loop(max(steps - 2, 0), steps)
     def _(i):
-        @pl.when(i + 1 < steps)
-        def _():
-            compute(0, i + 1)
-
         finish(0, i)
 
     for p in range(pieces):

time: 95.2 us -> 94.5 us (level)
  no operation moved by 1% of the time
where the time goes in v6:
time: 94.5 us; the launch traced here: 93.5 us
  Pallas kernels  89.1 us (94%)
  local copies, waits for them, and re-layouts  3.76 us (4%)
    pallas_call x1, Pallas kernels, on_device(): pl.pallas_call(functools.partial(mixer_kernel, n, n_seq, pieces, pc), out...  89.1 us
    unnamed x2, local copies, waits for them, and re-layouts  3.76 us

profile of v6, /device:TPU:8, one launch (start us, length us, event | category | flops | bytes accessed | tf_op | source)
XLA Modules:
  0.0 93.5 jit_solution(16806256072168287974)
XLA Ops:
  0.6 89.1 %shard_map.95 = (bf16[128,2048]{1,0:T(8,128)(2,1)}, bf16[128,2048]{1,0:T(8,128)(2,1)}) custom-call(bf16[128,2048]{1,0:T(8,128)(2,1)} %tokens.1, bf16[8192,2048]{1,0:T(8,128)(2,1)} %wg.1, bf16[8192,2048]{1,0:T(8,128)(2,1)} %wc.1, f32[4,2048]{1,0:T(4,128)} %cw.1, f32[1,2048]{1,0:T(1,128)} %bitcast.3, bf16[10,2048]{1,0:T(8,128)(2,1)} %sh.1, s32[1,128]{1,0:T(1,128)} %bitcast.4, ...), custom_call_target="tpu_custom_call" | custom-call | flops 17179869184 | bytes 33554432 | tf_op jit(solution)/shard_map/pallas_call | solution.py:484
  89.7 1.9 %copy.12 = bf16[128,2048]{1,0:T(8,128)(2,1)} copy(bf16[128,2048]{1,0:T(8,128)(2,1)} %get-tuple-element.4) | data formatting | bytes 1048576
  91.6 1.9 %copy.13 = bf16[128,2048]{1,0:T(8,128)(2,1)} copy(bf16[128,2048]{1,0:T(8,128)(2,1)} %get-tuple-element.5) | data formatting | bytes 1048576

commit v7 on v6

--- a/solution.py
+++ b/solution.py
@@ -16,16 +16,15 @@
     n, n_seq, pieces, pc,
     tokens, wg, wc, cw, cb, sh, tg, mk,
     gated, dtok,
-    tok_a, tok_b, w, acc, zx, grad, part, pair_in, chain_out, chain_in, gbuf, ohx, heads, obuf, tmp,
+    tok_a, w, acc, zx, grad, part, pair_in, chain_out, chain_in, gbuf, ohx, heads, obuf, tmp,
     w_sem, own_sem, up_sem, down_sem, z_recv, pair_sem, pair_recv,
     bp_sem, bp_recv, c_sem, c_recv, out_sem, misc,
 ):
     rows = tokens.shape[0]
     both = 2 * rows
-    hr = rows // 2
     ext = both + 2 * EDGE
-    size = (hr + EDGE, hr - EDGE)
-    toks = (tok_a, tok_b)
+    size = (rows,)
+    toks = (tok_a,)
     cols = acc.shape[1]
     half = cols // 2
     taps = cw.shape[0]
@@ -36,8 +35,6 @@
     has_low, has_high = z > 0, z < n - 1
     mine = pl.ds(pl.multiple_of(core * rows, rows), rows)
     other = pl.ds(pl.multiple_of((1 - core) * rows, rows), rows)
-    mine_h = pl.ds(pl.multiple_of(core * hr, hr), hr)
-    other_h = pl.ds(pl.multiple_of((1 - core) * hr, hr), hr)
     mine_d = pl.ds(pl.multiple_of(core * (pc // 2), pc // 2), pc // 2)
     other_d = pl.ds(pl.multiple_of((1 - core) * (pc // 2), pc // 2), pc // 2)
     my_cols = pl.ds(pl.multiple_of(core * half, half), half)
@@ -60,8 +57,7 @@
             copy.start()
 
     def own_src(q, p):
-        first = (1 - core) * size[1] if q == 0 else core * size[0]
-        return tokens.at[pl.ds(pl.multiple_of(first, EDGE), size[q]), pl.ds(pl.multiple_of(p * pc, pc), pc)]
+        return tokens.at[:, pl.ds(pl.multiple_of(p * pc, pc), pc)]
 
     def slot(q, j, p):
         return toks[q].at[j, p, pl.ds(pl.multiple_of(core * size[q], EDGE), size[q]), :]
@@ -136,10 +132,6 @@
             def _():
                 start_w(z + k, p)
 
-    for p in range(pieces):
-        own_copy(1, p).start()
-        pair_copy(own_src(1, p), 1, z, p).start()
-
     ids = lax.broadcasted_iota(jnp.int32, (LANES, rows), 0)
     picks = jnp.where((ids == tg[...]) & (mk[...] > 0), 1.0, 0.0)
     oh_mine[...] = jnp.transpose(picks).astype(ohx.dtype)
@@ -151,26 +143,17 @@
     ft = min(512, cols)
 
     def forward(q, j, p, first=False):
-        if q == 0:
-            for copy in w_copies(j, p):
-                copy.wait()
+        for copy in w_copies(j, p):
+            copy.wait()
 
         @pl.loop(0, cols // ft)
         def _(t):
             at = pl.ds(pl.multiple_of(t * ft, ft), ft)
             prod = jnp.dot(toks[q][j, p], w[j * pieces + p, :, at], preferred_element_type=jnp.float32)
-            if q == 0:
-                places = ((pl.ds(size[1], 2 * size[0]), prod),)
+            if first:
+                acc[:, at] = prod
             else:
-                places = (
-                    (pl.ds(0, size[1]), prod[: size[1]]),
-                    (pl.ds(both - size[1], size[1]), prod[size[1] :]),
-                )
-            for place, value in places:
-                if first:
-                    acc[place, at] = value
-                else:
-                    acc[place, at] += value
+                acc[:, at] += prod
 
     def own_forward(q, p):
         own_copy(q, p).wait()
@@ -221,17 +204,9 @@
 
     @pl.loop(1, n)
     def _(k):
-        @pl.when(k == n - 1)
-        def _():
-            send_own(1)
-
         for p in range(pieces):
             gather_step(0, k, p)
             multiply_step(0, k, p)
-
-            @pl.when(k == 1)
-            def _(p=p):
-                own_forward(1, p)
 
     def round_rows(first, count):
         @pl.loop(0, count // EDGE)
@@ -266,15 +241,13 @@
             dx += taps_w[k][None, :] * pltpu.roll(du, span - (taps - 1 - k), 0)
         return dz[inner], dx[inner]
 
-    def between(q, *windows, midway=None):
+    def between(q, *windows):
         @pl.loop(0, half // ct)
         def _(t):
             gcol = pl.ds(pl.multiple_of(t * ct, ct), ct)
             xcol = pl.ds(pl.multiple_of(half + t * ct, ct), ct)
             wcol = pl.ds(pl.multiple_of(core * half + t * ct, ct), ct)
             taps_w = cw[:, wcol]
-            if midway is not None:
-                pl.when(t == half // ct // 2)(midway)
             found = [window_values(e0, count, gcol, xcol, wcol, taps_w) for e0, count in windows]
             for at, values in ((gcol, [f[0] for f in found]), (xcol, [f[1] for f in found])):
                 value = values[0] if len(values) == 1 else jnp.concatenate(values, axis=0)
@@ -301,17 +274,12 @@
         ).wait_recv()
 
     def out_copies(q, p):
-        def place(to):
-            first = (1 - to) * hr if q == 0 else to * hr
-            return dtok.at[
-                pl.ds(pl.multiple_of(first, hr), hr), pl.ds(pl.multiple_of(p * pc + core * hd, hd), hd)
-            ]
-
+        place = dtok.at[:, pl.ds(pl.multiple_of(p * pc + core * hd, hd), hd)]
         return (
             remote(
-                obuf.at[q, p, other_h, :], place(1 - core), out_sem.at[q, p, 0], out_sem.at[q, p, 1], (partner, z)
+                obuf.at[q, p, other, :], place, out_sem.at[q, p, 0], out_sem.at[q, p, 1], (partner, z)
             ),
-            pltpu.make_async_copy(obuf.at[q, p, mine_h, :], place(core), out_sem.at[q, p, 2]),
+            pltpu.make_async_copy(obuf.at[q, p, mine, :], place, out_sem.at[q, p, 2]),
         )
 
     def backward(q, j, p):
@@ -368,42 +336,16 @@
 
     steps = (n - 1) * pieces
 
-    def at_step(act, i):
-        act(1, 1 + lax.div(i, pieces), lax.rem(i, pieces))
-
-    round_rows(size[1], 2 * size[0])
-    between(0, (hr, rows), midway=lambda: at_step(gather_step, jnp.int32(0)))
-    compute(0, jnp.int32(0))
-    at_step(multiply_step, jnp.int32(0))
-
-    @pl.loop(0, steps - 1)
-    def _(i):
-        @pl.when(i > 0)
-        def _():
-            finish(0, i - 1)
-
-        at_step(gather_step, i + 1)
-        compute(0, i + 1)
-        at_step(multiply_step, i + 1)
-
     round_rows(both - EDGE, EDGE)
     to_ahead.start()
     round_rows(0, EDGE)
     to_behind.start()
-    round_rows(EDGE, size[1] - EDGE)
-    round_rows(both - size[1], size[1] - EDGE)
-
-    @pl.loop(max(steps - 2, 0), steps)
-    def _(i):
-        finish(0, i)
-
-    for p in range(pieces):
-        backward(0, z, p)
+    round_rows(EDGE, both - 2 * EDGE)
     oh_edge.wait_recv()
     to_ahead.wait_recv()
     to_behind.wait_recv()
-    between(1, (0, hr), (ext - hr - 2 * EDGE, hr))
-    compute(1, jnp.int32(0))
+    between(0, (0, both))
+    compute(0, jnp.int32(0))
     g_local.start()
     g_pair.start()
 
@@ -428,21 +370,20 @@
     def _(i):
         @pl.when(i + 1 < steps)
         def _():
-            compute(1, i + 1)
-
-        finish(1, i)
+            compute(0, i + 1)
+
+        finish(0, i)
 
         @pl.when(i >= steps - pieces)
         def _():
-            own_sum(0, i - (steps - pieces))
-            backward(1, z, i - (steps - pieces))
+            backward(0, z, i - (steps - pieces))
 
     for p in range(pieces):
-        own_sum(1, p)
+        own_sum(0, p)
 
     @pl.loop(0, n)
     def _(j):
-        for q in range(2):
+        for q in range(1):
             for p in range(pieces):
                 @pl.when((j <= z) & has_high)
                 def _():
@@ -463,7 +404,7 @@
         copy.wait_send()
     g_local.wait()
     g_pair.wait()
-    for q in range(2):
+    for q in range(1):
         for p in range(pieces):
             for copy in out_copies(q, p):
                 copy.wait()
@@ -472,15 +413,14 @@
 def on_device(n, n_seq, tokens, w_gate, w_conv_in, conv_weight, conv_bias, score_head, targets, loss_mask):
     rows, block = tokens.shape
     d, chans = w_gate.shape
-    pc = min(2048, block)
+    pc = min(1024, block)
     pieces = block // pc
     bf16, f32 = jnp.bfloat16, jnp.float32
-    hr = rows // 2
     both = 2 * rows
     dma = pltpu.SemaphoreType.DMA
     vmem = pl.BlockSpec(memory_space=pltpu.VMEM)
     hbm = pl.BlockSpec(memory_space=pl.ANY)
-    per = (2, n, pieces)
+    per = (1, n, pieces)
     return pl.pallas_call(
         functools.partial(mixer_kernel, n, n_seq, pieces, pc),
         out_shape=(
@@ -490,26 +430,25 @@
         in_specs=[hbm, hbm, hbm, vmem, vmem, vmem, vmem, vmem],
         out_specs=(hbm, hbm),
         scratch_shapes=[
-            pltpu.VMEM((n, pieces, 2 * (hr + EDGE), pc), bf16),
-            pltpu.VMEM((n, pieces, 2 * (hr - EDGE), pc), bf16),
+            pltpu.VMEM((n, pieces, both, pc), bf16),
             pltpu.VMEM((n * pieces, pc, chans), bf16),
             pltpu.VMEM((both, chans), f32),
             pltpu.VMEM((both + 2 * EDGE, chans), bf16),
-            pltpu.VMEM((2, chans, rows), bf16),
-            pltpu.VMEM(per + (pc, rows), bf16),
-            pltpu.VMEM(per + (pc // 2, rows), bf16),
-            pltpu.VMEM(per + (pc // 2, rows), bf16),
-            pltpu.VMEM((2, n + 1, pieces, pc // 2, rows), bf16),
+            pltpu.VMEM((1, chans, both), bf16),
+            pltpu.VMEM(per + (pc, both), bf16),
+            pltpu.VMEM(per + (pc // 2, both), bf16),
+            pltpu.VMEM(per + (pc // 2, both), bf16),
+            pltpu.VMEM((1, n + 1, pieces, pc // 2, both), bf16),
             pltpu.VMEM((both, chans // 2), bf16),
             pltpu.VMEM((both + 2 * EDGE, LANES), bf16),
             pltpu.VMEM((LANES, chans // 2), bf16),
-            pltpu.VMEM((2, pieces, rows, pc // 2), bf16),
-            pltpu.VMEM((pc // 2, rows), f32),
+            pltpu.VMEM((1, pieces, both, pc // 2), bf16),
+            pltpu.VMEM((pc // 2, both), f32),
             dma((n * pieces, 2)),
-            dma((2, pieces)),
+            dma((1, pieces)),
             dma(per), dma(per), dma(per), dma(per), dma(per),
-            dma(per), dma(per), dma(per), dma((2, n + 1, pieces)),
-            dma((2, pieces, 3)),
+            dma(per), dma(per), dma(per), dma((1, n + 1, pieces)),
+            dma((1, pieces, 3)),
             dma((12,)),
         ],
         compiler_params=pltpu.CompilerParams(

time: 94.5 us -> 93.9 us (level)
  no operation moved by 1% of the time
where the time goes in v7:
time: 93.9 us; the launch traced here: 93.1 us
  Pallas kernels  88.7 us (94%)
  local copies, waits for them, and re-layouts  3.76 us (4%)
    pallas_call x1, Pallas kernels, on_device(): pl.pallas_call(functools.partial(mixer_kernel, n, n_seq, pieces, pc), out...  88.7 us
    unnamed x2, local copies, waits for them, and re-layouts  3.76 us

profile of v7, /device:TPU:8, one launch (start us, length us, event | category | flops | bytes accessed | tf_op | source)
XLA Modules:
  0.0 93.1 jit_solution(10783946597634119463)
XLA Ops:
  0.6 88.7 %shard_map.95 = (bf16[128,2048]{1,0:T(8,128)(2,1)}, bf16[128,2048]{1,0:T(8,128)(2,1)}) custom-call(bf16[128,2048]{1,0:T(8,128)(2,1)} %tokens.1, bf16[8192,2048]{1,0:T(8,128)(2,1)} %wg.1, bf16[8192,2048]{1,0:T(8,128)(2,1)} %wc.1, f32[4,2048]{1,0:T(4,128)} %cw.1, f32[1,2048]{1,0:T(1,128)} %bitcast.3, bf16[10,2048]{1,0:T(8,128)(2,1)} %sh.1, s32[1,128]{1,0:T(1,128)} %bitcast.4, ...), custom_call_target="tpu_custom_call" | custom-call | flops 17179869184 | bytes 33554432 | tf_op jit(solution)/shard_map/pallas_call | solution.py:424
  89.4 1.9 %copy.12 = bf16[128,2048]{1,0:T(8,128)(2,1)} copy(bf16[128,2048]{1,0:T(8,128)(2,1)} %get-tuple-element.4) | data formatting | bytes 1048576
  91.3 1.9 %copy.13 = bf16[128,2048]{1,0:T(8,128)(2,1)} copy(bf16[128,2048]{1,0:T(8,128)(2,1)} %get-tuple-element.5) | data formatting | bytes 1048576

commit v8 on v7

--- a/solution.py
+++ b/solution.py
@@ -413,7 +413,7 @@
 def on_device(n, n_seq, tokens, w_gate, w_conv_in, conv_weight, conv_bias, score_head, targets, loss_mask):
     rows, block = tokens.shape
     d, chans = w_gate.shape
-    pc = min(1024, block)
+    pc = min(2048, block)
     pieces = block // pc
     bf16, f32 = jnp.bfloat16, jnp.float32
     both = 2 * rows

time: 93.9 us -> 99.1 us (1.055)
  Pallas kernels: 88.7 us -> 93.7 us
    pallas_call x1, Pallas kernels: 88.7 us -> 93.7 us  [on_device(): pl.pallas_call(functools.partial(mixer_kernel, n, n_seq, pieces, pc), out...]
where the time goes in v8:
time: 99.1 us; the launch traced here: 98.2 us
  Pallas kernels  93.7 us (95%)
  local copies, waits for them, and re-layouts  3.76 us (4%)
    pallas_call x1, Pallas kernels, on_device(): pl.pallas_call(functools.partial(mixer_kernel, n, n_seq, pieces, pc), out...  93.7 us
    unnamed x2, local copies, waits for them, and re-layouts  3.76 us

profile of v8, /device:TPU:8, one launch (start us, length us, event | category | flops | bytes accessed | tf_op | source)
XLA Modules:
  0.0 98.2 jit_solution(18062051400798354053)
XLA Ops:
  0.6 93.7 %shard_map.95 = (bf16[128,2048]{1,0:T(8,128)(2,1)}, bf16[128,2048]{1,0:T(8,128)(2,1)}) custom-call(bf16[128,2048]{1,0:T(8,128)(2,1)} %tokens.1, bf16[8192,2048]{1,0:T(8,128)(2,1)} %wg.1, bf16[8192,2048]{1,0:T(8,128)(2,1)} %wc.1, f32[4,2048]{1,0:T(4,128)} %cw.1, f32[1,2048]{1,0:T(1,128)} %bitcast.3, bf16[10,2048]{1,0:T(8,128)(2,1)} %sh.1, s32[1,128]{1,0:T(1,128)} %bitcast.4, ...), custom_call_target="tpu_custom_call" | custom-call | flops 17179869184 | bytes 33554432 | tf_op jit(solution)/shard_map/pallas_call | solution.py:424
  94.4 1.9 %copy.12 = bf16[128,2048]{1,0:T(8,128)(2,1)} copy(bf16[128,2048]{1,0:T(8,128)(2,1)} %get-tuple-element.4) | data formatting | bytes 1048576
  96.3 1.9 %copy.13 = bf16[128,2048]{1,0:T(8,128)(2,1)} copy(bf16[128,2048]{1,0:T(8,128)(2,1)} %get-tuple-element.5) | data formatting | bytes 1048576
